TPU v7x, 32 devices: a whole 2x2x4 slice. The times are simulated.
32 devices in a mesh: group: 4 (over z), dev: 8 (over y, x, core).
Axes of the slice: x: 2, y: 2, z: 4, core: 2. Of those that a mesh axis runs over, the one named last changes fastest.
Arguments:
- points: bfloat16 [49152, 512], P(('group', 'dev')), may hold values from -5 to 5
- targets: float32 [8, 49152], P(None, ('group', 'dev')), may hold values from -16 to 16
- partner_tiles: int32 [4, 8, 4, 2], replicated, may hold values from -1 to 5, as said below
Outputs:
- solution: float32 [8, 49152], P(None, ('group', 'dev'))
- residual: float32 [8, 49152], P(None, ('group', 'dev'))
Inputs may be any that keep to these rules, and one draw needn't show every extreme that they name: `partner_tiles`: entry [g, v, h, c] names a tile of block (h, v) whose points are coupled with every point of block (g, v), or is -1. For one v and two groups at most one of the two blocks names tiles of the other, and no block names tiles of its own group. The tiles named in [g, v, h] are distinct and stand before its -1 entries. In every draw some block names 2 tiles of one other group.
All inputs are finite; a program needn't handle non-finite values.
Results may differ from a plain program's by a relative error of at most 0.0003.
Values may be sent and summed in bfloat16 or wider, within the bound.
A program may use at most 192 MiB of HBM per device.

v0:
```python
import jax
import jax.numpy as jnp
from jax import lax
from jax.sharding import PartitionSpec as P

TILE = 256
ITERS = 2


length_scale = 3.9
noise_level = 1.0
coupling_weight = 0.5
highest = lax.Precision.HIGHEST


def shifted(value, axis, steps):
    count = lax.axis_size(axis)
    leading, last = (max(0, -steps), min(count, count - steps))
    return lax.ppermute(value, axis, [(source, source + steps) for source in range(leading, last)])


def affinity(left_points, right_points, left_norms, right_norms):
    inner_prod = lax.dot_general(
        left_points, right_points, (((1,), (1,)), ((), ())), preferred_element_type=jnp.float32
    )
    dist_sq = jnp.maximum(left_norms[:, None] + right_norms[None, :] - 2.0 * inner_prod, 0.0)
    scaled = jnp.sqrt(dist_sq) / length_scale
    return jnp.maximum(1.0 - scaled, 0.0) ** 4 * (4.0 * scaled + 1.0)


def squares(values):
    return jnp.sum(jnp.square(values.astype(jnp.float32)), axis=1)


def contract_last(left_values, right_values):
    return lax.dot_general(
        left_values,
        right_values,
        (((1,), (1,)), ((), ())),
        precision=highest,
        preferred_element_type=jnp.float32,
    )


def move_points(values, offset):
    return shifted(values, "dev", offset)


def move_values(values, offset):
    return shifted(values.astype(jnp.bfloat16), "dev", offset).astype(values.dtype)


def trade_tiles(values):
    return lax.all_to_all(values, "group", split_axis=1, concat_axis=1, tiled=True)


def global_total(values):
    return lax.psum(values, ("group", "dev"))


def neighbours(values, strides, move_fn):
    collected = []
    for stride in strides:
        nearer = move_fn(values, stride)
        farther = move_fn(nearer, stride)
        collected.append((stride, nearer))
        collected.append((2 * stride, farther))
    return collected


def with_ones(values, needed):
    if needed:
        extra = jnp.ones((1,) + values.shape[1:], jnp.float32)
        return jnp.concatenate([values, extra], axis=0)
    return values


def on_device(points, targets, partner_tiles):
    row_count = points.shape[0]
    tile_count = row_count // TILE
    slot_width = partner_tiles.shape[3]
    group_count = lax.axis_size("group")
    dev_count = lax.axis_size("dev")
    group_index = lax.axis_index("group")
    position = lax.axis_index("dev")
    own_sq = squares(points)
    local_block = affinity(points, points, own_sq, own_sq)
    strides = (1,)
    band_blocks = []
    for offset, remote in neighbours(points, strides, move_points):
        source = position - offset
        inside = jnp.logical_and(source >= 0, source < dev_count).astype(jnp.float32)
        band_blocks.append((offset, affinity(points, remote, own_sq, squares(remote)) * inside))
    wanted = lax.dynamic_index_in_dim(
        lax.dynamic_index_in_dim(partner_tiles, group_index, 0, keepdims=False),
        position,
        0,
        keepdims=False,
    )
    by_position = lax.dynamic_index_in_dim(partner_tiles, position, 1, keepdims=False)
    requested = lax.dynamic_index_in_dim(by_position, group_index, 1, keepdims=False)
    slot_count = group_count * slot_width
    requested_flat = requested.reshape(slot_count)
    requested_index = jnp.maximum(requested_flat, 0)
    requested_live = requested_flat >= 0
    wanted_live = wanted.reshape(slot_count) >= 0
    requested_hot = jnp.logical_and(
        requested_index[:, None] == jnp.arange(tile_count)[None, :], requested_live[:, None]
    ).astype(jnp.float32)
    point_tiles = points.reshape(tile_count, TILE, points.shape[1])
    outgoing = jnp.where(
        requested_live[:, None, None],
        jnp.take(point_tiles, requested_index, axis=0),
        jnp.zeros((), points.dtype),
    )
    outgoing = outgoing.reshape(group_count, slot_width, TILE, points.shape[1])
    incoming = lax.all_to_all(outgoing, "group", split_axis=0, concat_axis=0, tiled=True).reshape(
        slot_count, TILE, points.shape[1]
    )

    def cross_fill(slot_index, stored):
        remote_tile = lax.dynamic_index_in_dim(incoming, slot_index, 0, keepdims=False)

        def compute():
            return affinity(points, remote_tile, own_sq, squares(remote_tile))

        def skipped():
            return jnp.zeros((row_count, TILE), jnp.float32)

        blocks = lax.cond(wanted_live[slot_index], compute, skipped)
        return lax.dynamic_update_index_in_dim(stored, blocks, slot_index, 0)

    cross_cache = lax.fori_loop(
        0, slot_count, cross_fill, jnp.zeros((slot_count, row_count, TILE), jnp.float32)
    )

    def couple(vector, with_degree):
        extended = with_ones(vector, with_degree)
        summed = contract_last(extended, local_block)
        remote_vectors = neighbours(vector, strides, move_values)
        for (offset, blocks), (same_offset, remote_vector) in zip(band_blocks, remote_vectors):
            summed = summed + contract_last(with_ones(remote_vector, with_degree), blocks)
            handed = jnp.dot(
                extended, blocks, precision=highest, preferred_element_type=jnp.float32
            )
            summed = summed + shifted(handed, "dev", -offset)
        probe_rows = vector.shape[0]
        tiled_vector = vector.reshape(probe_rows, tile_count, TILE)
        sending = (
            jnp.take(tiled_vector, requested_index, axis=1)
            * requested_live.astype(jnp.float32)[None, :, None]
        )
        arrived = trade_tiles(sending.reshape(probe_rows, group_count, slot_width, TILE)).reshape(
            probe_rows, slot_count, TILE
        )
        arrived = with_ones(arrived, with_degree)
        summed = summed + jnp.einsum("pst,srt->pr", arrived, cross_cache, precision=highest)
        extended_rows = extended.shape[0]
        handed_cross = jnp.einsum("pr,srt->pst", extended, cross_cache, precision=highest)
        returned = trade_tiles(
            handed_cross.reshape(extended_rows, group_count, slot_width, TILE)
        ).reshape(extended_rows, slot_count, TILE)
        gathered_back = jnp.einsum("pst,sq->pqt", returned, requested_hot, precision=highest)
        return summed + gathered_back.reshape(extended_rows, row_count)

    first_pass = couple(targets, True)
    degree = first_pass[-1]
    coupled = first_pass[:-1]

    def operate(vector, coupled_part):
        return noise_level * vector + coupling_weight * (degree[None, :] * vector - coupled_part)

    solution = jnp.zeros_like(targets)
    residual = targets
    direction = targets
    applied = operate(targets, coupled)
    first_sums = global_total(
        jnp.stack([jnp.sum(residual * residual, axis=1), jnp.sum(direction * applied, axis=1)])
    )
    norm_now = first_sums[0]
    curvature = first_sums[1]
    for iteration in range(ITERS):
        if iteration > 0:
            applied = operate(direction, couple(direction, False))
            curvature = global_total(jnp.sum(direction * applied, axis=1)[None, :])[0]
        step_size = norm_now / curvature
        solution = solution + step_size[:, None] * direction
        residual = residual - step_size[:, None] * applied
        if iteration + 1 < ITERS:
            norm_next = global_total(jnp.sum(residual * residual, axis=1)[None, :])[0]
            direction = residual + (norm_next / norm_now)[:, None] * direction
            norm_now = norm_next
    return (solution, residual)


def solution(mesh):
    return jax.shard_map(
        on_device,
        mesh=mesh,
        in_specs=(P(("group", "dev"), None), P(None, ("group", "dev")), P()),
        out_specs=(P(None, ("group", "dev")), P(None, ("group", "dev"))),
        check_vma=False,
    )
```

profile of v0, /device:TPU:0, one launch (start us, length us, event | category | flops | bytes accessed | tf_op | source)
XLA Modules:
  0.0 388.3 jit_solution(13417680495034091170)
XLA Ops:
  12.9 5.7 %all-to-all-start.1 = ((bf16[4,2,256,512]{3,2,1,0:T(8,128)(2,1)}), bf16[4,2,256,512]{3,2,1,0:T(8,128)(2,1)}, u32[]{:S(2)}, u32[]{:S(2)}) async-start(bf16[4,2,256,512]{3,2,1,0:T(8,128)(2,1)} %select_select_fusion), calls=%async_computation.1 | async-start | bytes 4194304 | tf_op jit(solution)/shard_map/all_to_all | solution.py:117
  21.4 9.4 %add_multiply_fusion = f32[1536,1536]{1,0:T(8,128)} fusion(bf16[1536,512]{1,0:T(8,128)(2,1)S(1)} %copy-done.3, f32[1536]{0:T(1024)S(1)} %multiply_reduce_fusion.3), kind=kOutput, calls=%fused_computation.19 | convolution fusion | flops 2444230656 | bytes 11016192 | tf_op jit(solution)/shard_map/dot_general | solution.py:23
  31.4 10.3 %fusion.22 = f32[9,1536]{1,0:T(8,128)S(1)} fusion(f32[1536,1536]{1,0:T(8,128)} %add_multiply_fusion, f32[8,1536]{1,0:T(8,128)S(1)} %copy-done.4), kind=kOutput, calls=%fused_computation.48 | convolution fusion | flops 254803968 | bytes 9541632 | tf_op jit(solution)/shard_map/dot_general | solution.py:36
  43.4 8.8 %multiply_multiply_fusion.1 = f32[1536,1536]{1,0:T(8,128)S(1)} fusion(f32[]{:T(128)S(6)} %convert_element_type.53, f32[1536]{0:T(1024)S(1)} %multiply_reduce_fusion.2, bf16[1536,512]{1,0:T(8,128)(2,1)S(1)} %copy-done.3, bf16[1536,512]{1,0:T(8,128)(2,1)} %collective-permute-done.1, f32[1536]{0:T(1024)S(1)} %multiply_reduce_fusion.3), kind=kOutput, calls=%fused_computation.18 | convolution fusion | flops 2446589952 | bytes 12595204 | tf_op jit(solution)/shard_map/dot_general | solution.py:23
  55.8 4.9 %fusion.20 = f32[9,1536]{1,0:T(8,128)S(1)} fusion(f32[1536,1536]{1,0:T(8,128)S(1)} %multiply_multiply_fusion.1, f32[8,1536]{1,0:T(8,128)S(1)} %copy-done.4), kind=kOutput, calls=%fused_computation.46 | convolution fusion | flops 254803968 | bytes 9541632 | tf_op jit(solution)/shard_map/dot_general | solution.py:143
  71.4 8.0 %fusion.10 = f32[9,1536]{1,0:T(8,128)S(1)} fusion(f32[9,1536]{1,0:T(8,128)S(1)} %collective-permute-done.2, f32[9,1536]{1,0:T(8,128)S(1)} %fusion.22, f32[1536,1536]{1,0:T(8,128)} %copy-done, bf16[8,1536]{1,0:T(8,128)(2,1)S(1)} %collective-permute-done), kind=kOutput, calls=%fused_computation.28 | convolution fusion | flops 254831616 | bytes 9627648 | tf_op jit(solution)/shard_map/dot_general | solution.py:36
  79.4 5.1 %all-to-all-start = ((f32[8,4,2,256]{3,0,2,1:T(8,128)}), f32[8,4,2,256]{3,0,2,1:T(8,128)S(1)}, u32[]{:S(2)}, u32[]{:S(2)}) async-start(f32[8,4,2,256]{3,0,2,1:T(8,128)} %bitcast.7), calls=%async_computation | async-start | bytes 131072 | tf_op jit(solution)/shard_map/all_to_all | solution.py:54
  84.5 35.0 %while.13 = (s32[]{:T(128)}, f32[8,1536,256]{1,2,0:T(8,128)}, pred[8]{0:T(512)(128)(4,1)S(1)}, f32[1536]{0:T(1024)S(1)}, bf16[8,256,512]{2,1,0:T(8,128)(2,1)}, /*index=5*/bf16[1536,512]{1,0:T(8,128)(2,1)S(1)}, s32[]{:T(128)}) while((s32[]{:T(128)}, f32[8,1536,256]{1,2,0:T(8,128)}, pred[8]{0:T(512)(128)(4,1)S(1)}, f32[1536]{0:T(1024)S(1)}, ...), condition=%wide.region_8.10_spmd, body=%wide.region_4.9_spmd.sunk | while | flops 407764736 | bytes 6825100 | solution.py:133
  119.4 13.1 %fusion.25 = f32[9,8,256]{2,0,1:T(8,128)S(1)} fusion(f32[8,1536,256]{1,2,0:T(8,128)} %get-tuple-element.143, f32[8,1536]{1,0:T(8,128)S(1)} %copy-done.4), kind=kOutput, calls=%fused_computation.51 | convolution fusion | flops 339738624 | bytes 12705792 | tf_op jit(solution)/shard_map/pr,srt->pst/dot_general | solution.py:159
  133.3 9.6 %all-to-all-start.2 = ((f32[9,4,2,256]{3,2,0,1:T(2,128)}), f32[9,4,2,256]{3,2,0,1:T(2,128)S(1)}, u32[]{:S(2)}, u32[]{:S(2)}) async-start(f32[9,4,2,256]{3,2,0,1:T(2,128)} %copy.19), calls=%async_computation.2 | async-start | bytes 147456 | tf_op jit(solution)/shard_map/all_to_all | solution.py:54
  142.9 9.0 %convolution_bitcast_fusion = f32[9,1536]{1,0:T(8,128)S(1)} fusion(f32[8,1536,256]{1,2,0:T(8,128)} %get-tuple-element.143, f32[8,8,256]{2,0,1:T(8,128)S(1)} %bitcast.105), kind=kOutput, calls=%fused_computation.29 | convolution fusion | flops 339738624 | bytes 12703744 | tf_op jit(solution)/shard_map/pst,srt->pr/dot_general | solution.py:157
  153.7 8.8 %multiply_multiply_fusion = f32[1536,1536]{1,0:T(8,128)S(1)} fusion(f32[]{:T(128)S(6)} %convert_element_type.55, f32[1536]{0:T(1024)S(1)} %multiply_reduce_fusion.1, bf16[1536,512]{1,0:T(8,128)(2,1)S(1)} %get-tuple-element.226, bf16[1536,512]{1,0:T(8,128)(2,1)} %collective-permute-done.4, f32[1536]{0:T(1024)S(1)} %get-tuple-element.249), kind=kOutput, calls=%fused_computation.17 | convolution fusion | flops 2446589952 | bytes 12595204 | tf_op jit(solution)/shard_map/dot_general | solution.py:23
  166.1 4.7 %fusion.18 = f32[9,1536]{1,0:T(8,128)S(1)} fusion(f32[1536,1536]{1,0:T(8,128)S(1)} %multiply_multiply_fusion, f32[8,1536]{1,0:T(8,128)S(1)} %copy-done.4), kind=kOutput, calls=%fused_computation.44 | convolution fusion | flops 254803968 | bytes 9541632 | tf_op jit(solution)/shard_map/dot_general | solution.py:143
  172.4 5.4 %collective-permute-done.5 = f32[9,1536]{1,0:T(8,128)S(1)} collective-permute-done((f32[9,1536]{1,0:T(8,128)S(1)}, f32[9,1536]{1,0:T(8,128)S(1)}, u32[]{:S(2)}, u32[]{:S(2)}) %collective-permute-start.5) | collective-permute-done | bytes 55328 | tf_op jit(solution)/shard_map/ppermute | solution.py:19
  177.9 8.0 %fusion.9 = f32[9,1536]{1,0:T(8,128)S(1)} fusion(f32[9,1536]{1,0:T(8,128)S(1)} %bitcast.104, f32[9,1536]{1,0:T(8,128)S(1)} %convolution_bitcast_fusion, f32[9,1536]{1,0:T(8,128)S(1)} %collective-permute-done.5, f32[9,1536]{1,0:T(8,128)S(1)} %fusion.10, f32[1536,1536]{1,0:T(8,128)} %copy-done.1, bf16[8,1536]{1,0:T(8,128)(2,1)S(1)} %collective-permute-done.3), kind=kOutput, calls=%fused_computation.26 | convolution fusion | flops 254859264 | bytes 9738240 | tf_op jit(solution)/shard_map/dot_general | solution.py:36
  186.0 40.4 %psum.21 = f32[2,8]{1,0:T(2,128)S(1)} all-reduce(f32[2,8]{1,0:T(2,128)S(1)} %pad_maximum_fusion), channel_id=1, replica_groups=mesh['group'=4,'dev'=8] {'group','dev'}, use_global_device_ids=true, to_apply=%region_10.12 | all-reduce | flops 16 | bytes 128 | tf_op jit(solution)/shard_map/psum | solution.py:58
  226.6 41.4 %psum.22 = f32[1,8]{1,0:T(1,128)S(1)} all-reduce(f32[1,8]{1,0:T(1,128)S(1)} %bitcast.112), channel_id=1, replica_groups=mesh['group'=4,'dev'=8] {'group','dev'}, use_global_device_ids=true, to_apply=%region_12.14 | all-reduce | flops 8 | bytes 64 | tf_op jit(solution)/shard_map/psum | solution.py:58
  268.2 14.2 %fusion.29 = f32[8,8,256]{2,0,1:T(8,128)} fusion(f32[8,1536,256]{1,2,0:T(8,128)} %get-tuple-element.143, f32[8,1536]{1,0:T(8,128)S(1)} %get-tuple-element.161), kind=kOutput, calls=%fused_computation.58 | convolution fusion | flops 301989888 | bytes 12697600 | tf_op jit(solution)/shard_map/pr,srt->pst/dot_general | solution.py:159
  291.5 10.1 %fusion.50 = f32[8,1536]{1,0:T(8,128)S(1)} fusion(f32[8,1536]{1,0:T(8,128)S(1)} %get-tuple-element.161, f32[1536,1536]{1,0:T(8,128)} %add_multiply_fusion), kind=kOutput, calls=%fused_computation.99 | convolution fusion | flops 226492416 | bytes 9535488 | tf_op jit(solution)/shard_map/dot_general | solution.py:36
  315.8 7.9 %fusion.17 = f32[8,1536]{1,0:T(8,128)S(1)} fusion(f32[8,1536]{1,0:T(8,128)S(1)} %collective-permute-done.7, f32[8,1536]{1,0:T(8,128)S(1)} %fusion.50, bf16[8,1536]{1,0:T(8,128)(2,1)S(1)} %collective-permute-done.6, f32[1536,1536]{1,0:T(8,128)} %copy-done), kind=kOutput, calls=%fused_computation.38 | convolution fusion | flops 226516992 | bytes 9609216 | tf_op jit(solution)/shard_map/dot_general | solution.py:36
  323.7 4.8 %all-to-all-start.4 = ((f32[8,4,2,256]{3,0,2,1:T(8,128)}), f32[8,4,2,256]{3,0,2,1:T(8,128)S(1)}, u32[]{:S(2)}, u32[]{:S(2)}) async-start(f32[8,4,2,256]{3,0,2,1:T(8,128)} %bitcast.27), calls=%async_computation.4 | async-start | bytes 131072 | tf_op jit(solution)/shard_map/all_to_all | solution.py:54
  328.5 8.9 %convolution_bitcast_fusion.1 = f32[8,1536]{1,0:T(8,128)S(1)} fusion(f32[8,8,256]{2,0,1:T(8,128)S(1)} %bitcast.106, f32[8,1536,256]{1,2,0:T(8,128)} %get-tuple-element.143), kind=kOutput, calls=%fused_computation.39 | convolution fusion | flops 301989888 | bytes 12697600 | tf_op jit(solution)/shard_map/pst,srt->pr/dot_general | solution.py:157
  337.6 8.0 %multiply_reduce_fusion.4 = (f32[8]{0:T(128)S(1)}, f32[8,1536]{1,0:T(8,128)S(1)}) fusion(f32[8,1536]{1,0:T(8,128)S(1)} %get-tuple-element.161, f32[8,1536]{1,0:T(8,128)S(1)} %bitcast.108, f32[8,1536]{1,0:T(8,128)S(1)} %convolution_bitcast_fusion.1, f32[8,1536]{1,0:T(8,128)S(1)} %collective-permute-done.9, f32[8,1536]{1,0:T(8,128)S(1)} %fusion.17, ...), kind=kOutput, calls=%fused_computation.62 | convolution fusion | flops 226615296 | bytes 9762848 | tf_op jit(solution)/shard_map/dot_general | solution.py:36
  345.7 41.7 %psum.23 = f32[1,8]{1,0:T(1,128)S(1)} all-reduce(f32[1,8]{1,0:T(1,128)S(1)} %bitcast.111), channel_id=1, replica_groups=mesh['group'=4,'dev'=8] {'group','dev'}, use_global_device_ids=true, to_apply=%region_14.16 | all-reduce | flops 8 | bytes 64 | tf_op jit(solution)/shard_map/psum | solution.py:58
  (119 shorter events, 107.2 us)
Async XLA Ops:
  0.6 20.3 %copy-start.3 = (bf16[1536,512]{1,0:T(8,128)(2,1)S(1)}, bf16[1536,512]{1,0:T(8,128)(2,1)}, u32[]{:S(2)}) copy-start(bf16[1536,512]{1,0:T(8,128)(2,1)} %param.9) | copy-start | bytes 4718596
  0.6 18.0 %copy-start.4 = (f32[8,1536]{1,0:T(8,128)S(1)}, f32[8,1536]{1,0:T(8,128)}, u32[]{:S(2)}) copy-start(f32[8,1536]{1,0:T(8,128)} %param.10) | copy-start | bytes 147460
  0.7 41.0 %collective-permute-start.1 = (bf16[1536,512]{1,0:T(8,128)(2,1)}, bf16[1536,512]{1,0:T(8,128)(2,1)}, u32[]{:S(2)}, u32[]{:S(2)}) collective-permute-start(bf16[1536,512]{1,0:T(8,128)(2,1)} %param.9), channel_id=1, source_target_pairs={{0,1},{1,2},{2,3},{3,4},{4,5},{5,6},{6,7},{8,9},{9,10},{10,11},{11... | collective-permute-start | bytes 4718600 | tf_op jit(solution)/shard_map/ppermute | solution.py:19
  12.9 66.4 %all-to-all-start.1 = ((bf16[4,2,256,512]{3,2,1,0:T(8,128)(2,1)}), bf16[4,2,256,512]{3,2,1,0:T(8,128)(2,1)}, u32[]{:S(2)}, u32[]{:S(2)}) async-start(bf16[4,2,256,512]{3,2,1,0:T(8,128)(2,1)} %select_select_fusion), calls=%async_computation.1 | async-start | bytes 4194304 | tf_op jit(solution)/shard_map/all_to_all | solution.py:117
  18.6 45.1 %collective-permute-start = (bf16[8,1536]{1,0:T(8,128)(2,1)S(1)}, bf16[8,1536]{1,0:T(8,128)(2,1)S(1)}, u32[]{:S(2)}, u32[]{:S(2)}) collective-permute-start(bf16[8,1536]{1,0:T(8,128)(2,1)S(1)} %convert_element_type.51), channel_id=1, source_target_pairs={{0,1},{1,2},{2,3},{3,4},{4,5},{5,6},{6,7},{8,9},{9,10},{10,11},{11... | collective-permute-start | bytes 73736 | tf_op jit(solution)/shard_map/ppermute | solution.py:19
  52.3 3.6 copy-start
  60.8 10.6 %collective-permute-start.2 = (f32[9,1536]{1,0:T(8,128)S(1)}, f32[9,1536]{1,0:T(8,128)S(1)}, u32[]{:S(2)}, u32[]{:S(2)}) collective-permute-start(f32[9,1536]{1,0:T(8,128)S(1)} %fusion.20), channel_id=1, source_target_pairs={{1,0},{2,1},{3,2},{4,3},{5,4},{6,5},{7,6},{9,8},{10,9},{11,10},{12... | collective-permute-start | bytes 165896 | tf_op jit(solution)/shard_map/ppermute | solution.py:19
  63.7 108.7 %collective-permute-start.3 = (bf16[8,1536]{1,0:T(8,128)(2,1)S(1)}, bf16[8,1536]{1,0:T(8,128)(2,1)S(1)}, u32[]{:S(2)}, u32[]{:S(2)}) collective-permute-start(bf16[8,1536]{1,0:T(8,128)(2,1)S(1)} %collective-permute-done), channel_id=1, source_target_pairs={{0,1},{1,2},{2,3},{3,4},{4,5},{5,6},{6,7},{8,9},{9,10},{10,11},{11... | collective-permute-start | bytes 73736 | tf_op jit(solution)/shard_map/ppermute | solution.py:19
  66.8 85.1 %collective-permute-start.4 = (bf16[1536,512]{1,0:T(8,128)(2,1)}, bf16[1536,512]{1,0:T(8,128)(2,1)}, u32[]{:S(2)}, u32[]{:S(2)}) collective-permute-start(bf16[1536,512]{1,0:T(8,128)(2,1)} %collective-permute-done.1), channel_id=1, source_target_pairs={{0,1},{1,2},{2,3},{3,4},{4,5},{5,6},{6,7},{8,9},{9,10},{10,11},{11... | collective-permute-start | bytes 4718600 | tf_op jit(solution)/shard_map/ppermute | solution.py:19
  79.4 53.9 %all-to-all-start = ((f32[8,4,2,256]{3,0,2,1:T(8,128)}), f32[8,4,2,256]{3,0,2,1:T(8,128)S(1)}, u32[]{:S(2)}, u32[]{:S(2)}) async-start(f32[8,4,2,256]{3,0,2,1:T(8,128)} %bitcast.7), calls=%async_computation | async-start | bytes 131072 | tf_op jit(solution)/shard_map/all_to_all | solution.py:54
  133.3 38.8 %all-to-all-start.2 = ((f32[9,4,2,256]{3,2,0,1:T(2,128)}), f32[9,4,2,256]{3,2,0,1:T(2,128)S(1)}, u32[]{:S(2)}, u32[]{:S(2)}) async-start(f32[9,4,2,256]{3,2,0,1:T(2,128)} %copy.19), calls=%async_computation.2 | async-start | bytes 147456 | tf_op jit(solution)/shard_map/all_to_all | solution.py:54
  162.5 3.6 copy-start.1
  170.8 7.1 %collective-permute-start.5 = (f32[9,1536]{1,0:T(8,128)S(1)}, f32[9,1536]{1,0:T(8,128)S(1)}, u32[]{:S(2)}, u32[]{:S(2)}) collective-permute-start(f32[9,1536]{1,0:T(8,128)S(1)} %fusion.18), channel_id=1, source_target_pairs={{2,0},{3,1},{4,2},{5,3},{6,4},{7,5},{10,8},{11,9},{12,10},{13,11},... | collective-permute-start | bytes 165896 | tf_op jit(solution)/shard_map/ppermute | solution.py:19
  268.1 14.4 %copy-start.2 = (f32[1536,1536]{1,0:T(8,128)S(1)}, f32[1536,1536]{1,0:T(8,128)}, u32[]{:S(2)}) copy-start(f32[1536,1536]{1,0:T(8,128)} %copy-done.1) | copy-start | bytes 28311556
  268.2 18.8 %slice-start = ((s8[9437184]{0:T(1024)(128)(4,1)}), s8[4194304]{0:T(1024)(128)(4,1)S(1)}, s32[]{:S(2)}) async-start(s8[9437184]{0:T(1024)(128)(4,1)} %bitcast.96), calls=%async_computation.5 | async-start | bytes 8388608
  268.2 18.8 %slice-start.1 = ((s8[9437184]{0:T(1024)(128)(4,1)}), s8[4194304]{0:T(1024)(128)(4,1)S(1)}, s32[]{:S(2)}) async-start(s8[9437184]{0:T(1024)(128)(4,1)} %bitcast.96), calls=%async_computation.6 | async-start | bytes 8388608
  282.4 4.5 %slice-start.2 = ((s8[9437184]{0:T(1024)(128)(4,1)}), s8[1048576]{0:T(1024)(128)(4,1)S(1)}, s32[]{:S(2)}) async-start(s8[9437184]{0:T(1024)(128)(4,1)} %bitcast.96), calls=%async_computation.7 | async-start | bytes 2097152
  302.2 13.6 %collective-permute-start.7 = (f32[8,1536]{1,0:T(8,128)S(1)}, f32[8,1536]{1,0:T(8,128)S(1)}, u32[]{:S(2)}, u32[]{:S(2)}) collective-permute-start(f32[8,1536]{1,0:T(8,128)S(1)} %fusion.51), channel_id=1, source_target_pairs={{1,0},{2,1},{3,2},{4,3},{5,4},{6,5},{7,6},{9,8},{10,9},{11,10},{12... | collective-permute-start | bytes 147464 | tf_op jit(solution)/shard_map/ppermute | solution.py:19
  303.5 8.6 %collective-permute-start.6 = (bf16[8,1536]{1,0:T(8,128)(2,1)S(1)}, bf16[8,1536]{1,0:T(8,128)(2,1)S(1)}, u32[]{:S(2)}, u32[]{:S(2)}) collective-permute-start(bf16[8,1536]{1,0:T(8,128)(2,1)S(1)} %get-tuple-element.160), channel_id=1, source_target_pairs={{0,1},{1,2},{2,3},{3,4},{4,5},{5,6},{6,7},{8,9},{9,10},{10,11},{11... | collective-permute-start | bytes 73736 | tf_op jit(solution)/shard_map/ppermute | solution.py:19
  307.2 16.5 %all-to-all-start.3 = ((f32[8,4,2,256]{3,0,2,1:T(8,128)}), f32[8,4,2,256]{3,0,2,1:T(8,128)S(1)}, u32[]{:S(2)}, u32[]{:S(2)}) async-start(f32[8,4,2,256]{3,0,2,1:T(8,128)} %bitcast.23), calls=%async_computation.3 | async-start | bytes 131072 | tf_op jit(solution)/shard_map/all_to_all | solution.py:54
  310.8 26.8 %collective-permute-start.9 = (f32[8,1536]{1,0:T(8,128)S(1)}, f32[8,1536]{1,0:T(8,128)S(1)}, u32[]{:S(2)}, u32[]{:S(2)}) collective-permute-start(f32[8,1536]{1,0:T(8,128)S(1)} %fusion.52), channel_id=1, source_target_pairs={{2,0},{3,1},{4,2},{5,3},{6,4},{7,5},{10,8},{11,9},{12,10},{13,11},... | collective-permute-start | bytes 147464 | tf_op jit(solution)/shard_map/ppermute | solution.py:19
  312.1 25.5 %collective-permute-start.8 = (bf16[8,1536]{1,0:T(8,128)(2,1)S(1)}, bf16[8,1536]{1,0:T(8,128)(2,1)S(1)}, u32[]{:S(2)}, u32[]{:S(2)}) collective-permute-start(bf16[8,1536]{1,0:T(8,128)(2,1)S(1)} %collective-permute-done.6), channel_id=1, source_target_pairs={{0,1},{1,2},{2,3},{3,4},{4,5},{5,6},{6,7},{8,9},{9,10},{10,11},{11... | collective-permute-start | bytes 73736 | tf_op jit(solution)/shard_map/ppermute | solution.py:19
  323.7 13.6 %all-to-all-start.4 = ((f32[8,4,2,256]{3,0,2,1:T(8,128)}), f32[8,4,2,256]{3,0,2,1:T(8,128)S(1)}, u32[]{:S(2)}, u32[]{:S(2)}) async-start(f32[8,4,2,256]{3,0,2,1:T(8,128)} %bitcast.27), calls=%async_computation.4 | async-start | bytes 131072 | tf_op jit(solution)/shard_map/all_to_all | solution.py:54
where the time goes:
time: 396 us; the launch traced here: 388 us
  matrix products  152 us (38%)
  blocking collectives  124 us (31%)
  starting transfers between devices  54.2 us (14%)
  local copies, waits for them, and re-layouts  28.9 us (7%)
  other arithmetic  16.9 us (4%)
  loops' own time  5.66 us (1%)
  waiting for transfers between devices  5.5 us (1%)
    psum x3, blocking collectives, global_total(): return lax.psum(values, ('group', 'dev'))  124 us
    dot_general x6, matrix products, contract_last(): lax.dot_general(left_values, right_values, (((1,), (1,)), ((), ())), prec...  52.2 us
    dot_general x7, matrix products, affinity(): lax.dot_general(left_points, right_points, (((1,), (1,)), ((), ())), pref...  35.9 us
    dot_general x2, matrix products, couple(): jnp.einsum('pr,srt->pst', extended, cross_cache, precision=highest)  27.4 us
    ppermute x10, starting transfers between devices, shifted(): lax.ppermute(value, axis, [(source, source + steps) for source in range(l...  25.4 us
    all_to_all x4, starting transfers between devices, trade_tiles(): lax.all_to_all(values, 'group', split_axis=1, concat_axis=1, tiled=True)  23.1 us
    dot_general x4, matrix products, couple(): jnp.dot(extended, blocks, precision=highest, preferred_element_type=jnp.f...  18.7 us
    dot_general x2, matrix products, couple(): jnp.einsum('pst,srt->pr', arrived, cross_cache, precision=highest)  17.9 us
  transfers between devices with their start and end apart: 15, of which 1 were waited for; matrix products, arithmetic and copies ran while one was open for 36% of the time, Pallas kernels for 0%

commit v1 on v0

v1 whole, which is shorter than its diff:
```python
import functools

import jax
import jax.numpy as jnp
from jax import lax
from jax.experimental import pallas as pl
from jax.experimental.pallas import tpu as pltpu
from jax.sharding import PartitionSpec as P

TILE = 256

length_scale = 3.9
noise_level = 1.0
coupling_weight = 0.5
MESH = pl.DeviceIdType.MESH
NT = (((1,), (1,)), ((), ()))
NN = (((1,), (0,)), ((), ()))


def mxu(left, right, dims):
    return lax.dot_general(left, right, dims, preferred_element_type=jnp.float32)


def split_rows(values, ones):
    high = values.astype(jnp.bfloat16).astype(jnp.float32)
    pieces = [high, values - high]
    if ones:
        pieces += [jnp.ones_like(values), jnp.zeros_like(values)]
    return jnp.concatenate(pieces, axis=0).astype(jnp.bfloat16)


def merge_rows(summed, probes, ones):
    coupled = summed[0:probes] + summed[probes : 2 * probes]
    if ones:
        return jnp.concatenate([coupled, summed[2 * probes : 3 * probes]], axis=0)
    return coupled


def kernel(groups, devs, cap, probes, tiles,
           tab, pts, tgt, sol, res,
           pin, outp, inp, kmat, kc, ncol, vec1, vin1, cvo1, cvi1, vec2, vin2, cvo2, cvi2,
           hout1, hin1, cho1, chi1, hout2, hin2, cho2, chi2,
           mown, mtile, mrem, mc, acc, red1o, red1, red2o, red2,
           psend, precv, cpsend, cprecv, vsend, vrecv, cvsend, cvrecv,
           hsend, hrecv, chsend, chrecv, r1send, r1recv, r2send, r2recv):
    g = lax.axis_index("group")
    d = lax.axis_index("dev")
    par = lax.rem(d, 2)
    odd = par == 1
    even = par == 0
    peers = groups - 1
    cols = tiles * TILE

    def tile_id(owner, other, c):
        return tab[((owner * devs + d) * groups + other) * cap + c]

    def up(k):
        return lax.rem(g + k, groups)

    def down(k):
        return lax.rem(g + groups - k, groups)

    def cs(j):
        return slice(j * TILE, (j + 1) * TILE)

    @pl.loop(0, tiles)
    def _(i):
        wide = pts[i].astype(jnp.float32)
        ncol[i] = jnp.sum(wide * wide, axis=1, keepdims=True)

    for j in range(tiles):
        wide = pts[j].astype(jnp.float32)
        squares = wide * wide
        high = squares.astype(jnp.bfloat16)
        low = (squares - high.astype(jnp.float32)).astype(jnp.bfloat16)
        ones = jnp.ones((16, wide.shape[1]), jnp.bfloat16)
        sums = mxu(ones, high, NT) + mxu(ones, low, NT)
        vec1[0:probes, cs(j)] = tgt[:, cs(j)]
        vec1[probes : 2 * probes, cs(j)] = sums[0:probes]
        rows = split_rows(tgt[:, cs(j)], True)
        mown[:, cs(j)] = rows
        mtile[j] = rows
    for k in range(1, groups):
        for c in range(cap):
            named = tile_id(up(k), g, c)
            outp[k - 1, c] = pts[jnp.maximum(named, 0)]
            total = jnp.zeros((2 * probes, TILE), jnp.float32)
            for q in range(tiles):
                total = total + jnp.where(named == q, 1.0, 0.0) * vec1[:, cs(q)]
            cvo1[k - 1, :, cs(c)] = total

    barrier = pltpu.get_barrier_semaphore()
    for k in range(1, groups):
        pl.semaphore_signal(barrier, inc=1, device_id={"group": up(k)}, device_id_type=MESH)
    for k in range(1, devs):
        pl.semaphore_signal(barrier, inc=1, device_id={"dev": lax.rem(d + k, devs)}, device_id_type=MESH)
    pl.semaphore_wait(barrier, groups + devs - 2)

    def remote(src, dst, ssem, rsem, where):
        return pltpu.make_async_remote_copy(
            src_ref=src, dst_ref=dst, send_sem=ssem, recv_sem=rsem, device_id=where, device_id_type=MESH
        )

    has_next = d + 1 < devs
    far = jnp.where(odd, jnp.minimum(d + 2, devs - 1), jnp.maximum(d - 2, 0))
    has_far = jnp.logical_or(jnp.logical_and(odd, d + 2 < devs), jnp.logical_and(even, d >= 2))
    nxt = jnp.minimum(d + 1, devs - 1)
    has_first = jnp.logical_or(odd, d + 2 < devs)
    has_second = d >= 2
    first_owner = jnp.where(odd, jnp.maximum(d - 1, 0), jnp.minimum(d + 2, devs - 1))
    second_owner = jnp.where(odd, jnp.maximum(d - 2, 0), jnp.maximum(d - 1, 0))
    has_block = (has_first, has_second)
    block_owner = (first_owner, second_owner)
    block_slot = (1 - par, par)

    def vec_copy(r, which):
        src, dst = (vec1, vin1) if r == 0 else (vec2, vin2)
        return remote(src, dst.at[par], vsend.at[r, which], vrecv.at[r, par], {"dev": (nxt, far)[which]})

    def vec_in(r, block):
        src, dst = (vec1, vin1) if r == 0 else (vec2, vin2)
        return remote(src, dst.at[block], vsend.at[r, 0], vrecv.at[r, block], {"dev": nxt})

    def cvec(r, k):
        src, dst = (cvo1, cvi1) if r == 0 else (cvo2, cvi2)
        return remote(src.at[k - 1], dst.at[k - 1], cvsend.at[r, k - 1], cvrecv.at[r, k - 1], {"group": up(k)})

    def hand(r, block):
        src, dst = (hout1, hin1) if r == 0 else (hout2, hin2)
        slot = block_slot[block]
        return remote(src.at[block], dst.at[slot], hsend.at[r, block], hrecv.at[r, slot],
                      {"dev": block_owner[block]})

    def hand_in(r, slot):
        src, dst = (hout1, hin1) if r == 0 else (hout2, hin2)
        return remote(src.at[0], dst.at[slot], hsend.at[r, 0], hrecv.at[r, slot], {"dev": nxt})

    def chand(r, k):
        src, dst = (cho1, chi1) if r == 0 else (cho2, chi2)
        return remote(src.at[k - 1], dst.at[k - 1], chsend.at[r, k - 1], chrecv.at[r, k - 1], {"group": down(k)})

    def cpts(k):
        return remote(outp.at[k - 1], inp.at[k - 1], cpsend.at[k - 1], cprecv.at[k - 1], {"group": up(k)})

    far_pts = remote(pts, pin.at[par], psend.at[1], precv.at[par], {"dev": far})
    mate_pts = remote(pts, pin.at[0], psend.at[0], precv.at[0], {"dev": nxt})
    forward_pts = remote(pin.at[1], pin.at[1], psend.at[0], precv.at[1], {"dev": jnp.maximum(d - 1, 0)})

    def send_vectors(r):
        for which, cond in ((0, has_next), (1, has_far)):
            @pl.when(cond)
            def _():
                vec_copy(r, which).start()
        for k in range(1, groups):
            cvec(r, k).start()

    send_vectors(0)
    for k in range(1, groups):
        cpts(k).start()

    @pl.when(has_far)
    def _():
        far_pts.start()

    @pl.when(even)
    def _():
        mate_pts.start()

    def affinity(own, norm_col, other, norm_row):
        inner = mxu(own, other, NT)
        dist_sq = jnp.maximum(norm_col + norm_row - 2.0 * inner, 0.0)
        scaled = dist_sq * lax.rsqrt(jnp.maximum(dist_sq, 1e-30)) * (1.0 / length_scale)
        near = jnp.maximum(1.0 - scaled, 0.0)
        near = near * near
        return near * near * (4.0 * scaled + 1.0)

    @pl.loop(0, tiles)
    def _(i):
        total = jnp.zeros((4 * probes, TILE), jnp.float32)
        for j in range(tiles):
            value = affinity(pts[i], ncol[i], pts[j], vec1[probes : probes + 1, cs(j)]).astype(jnp.bfloat16)
            kmat[0, i, :, cs(j)] = value
            total = total + mxu(mown[:, cs(j)], value, NT)
        acc[i] = total

    def band(block):
        vec_in(0, block).wait_recv()
        for j in range(tiles):
            mrem[:, cs(j)] = split_rows(vin1[block, 0:probes, cs(j)], True)
        hout1[block] = jnp.zeros((2 * probes, cols), jnp.float32)

        @pl.loop(0, tiles)
        def _(i):
            total = acc[i]
            for j in range(tiles):
                value = affinity(
                    pts[i], ncol[i], pin[block, j], vin1[block, probes : probes + 1, cs(j)]
                ).astype(jnp.bfloat16)
                kmat[1 + block, i, :, cs(j)] = value
                total = total + mxu(mrem[:, cs(j)], value, NT)
                hout1[block, :, cs(j)] += merge_rows(mxu(mtile[i], value, NN), probes, True)
            acc[i] = total

        hand(0, block).start()

    def cross(k):
        cvec(0, k).wait_recv()
        cpts(k).wait_recv()
        live = [jnp.where(tile_id(g, down(k), c) >= 0, 1.0, 0.0) for c in range(cap)]
        for c in range(cap):
            mc[k - 1, :, cs(c)] = split_rows(cvi1[k - 1, 0:probes, cs(c)], True)
        cho1[k - 1] = jnp.zeros((2 * probes, cap * TILE), jnp.float32)

        @pl.loop(0, tiles)
        def _(i):
            total = acc[i]
            for c in range(cap):
                value = affinity(
                    pts[i], ncol[i], inp[k - 1, c], cvi1[k - 1, probes : probes + 1, cs(c)]
                )
                value = (value * live[c]).astype(jnp.bfloat16)
                kc[k - 1, i, :, cs(c)] = value
                total = total + mxu(mc[k - 1, :, cs(c)], value, NT)
                cho1[k - 1, :, cs(c)] += merge_rows(mxu(mtile[i], value, NN), probes, True)
            acc[i] = total

        chand(0, k).start()

    @pl.when(has_first)
    def _():
        remote(pts, pin.at[0], psend.at[0], precv.at[0], {"dev": nxt}).wait_recv()
        band(0)

    cross(1)

    @pl.when(has_second)
    def _():
        remote(pts, pin.at[1], psend.at[0], precv.at[1], {"dev": nxt}).wait_recv()

        @pl.when(odd)
        def _():
            forward_pts.start()

        band(1)

    for k in range(2, groups):
        cross(k)

    def gather_backs(r, total):
        incoming, cross_in = (hin1, chi1) if r == 0 else (hin2, chi2)
        for k in range(1, groups):
            chand(r, k).wait_recv()
        for k in range(1, groups):
            for c in range(cap):
                named = tile_id(up(k), g, c)
                part = cross_in[k - 1, :, cs(c)]
                for q in range(tiles):
                    total[q] = total[q] + jnp.where(named == q, 1.0, 0.0) * part
        return total

    def wait_hands(r):
        for slot, cond in ((0, has_next), (1, has_far)):
            @pl.when(cond)
            def _():
                hand_in(r, slot).wait_recv()

    incoming_ok = [jnp.where(has_next, 1.0, 0.0), jnp.where(has_far, 1.0, 0.0)]
    for slot, cond in ((0, has_next), (1, has_far)):
        @pl.when(jnp.logical_not(cond))
        def _():
            hin1[slot] = jnp.zeros((2 * probes, cols), jnp.float32)
            hin2[slot] = jnp.zeros((probes, cols), jnp.float32)

    wait_hands(0)
    sums = [merge_rows(acc[q], probes, True) + hin1[0, :, cs(q)] + hin1[1, :, cs(q)] for q in range(tiles)]
    sums = gather_backs(0, sums)
    for q in range(tiles):
        base = tgt[:, cs(q)]
        degree = sums[q][probes : 2 * probes]
        applied = noise_level * base + coupling_weight * (degree * base - sums[q][0:probes])
        vec2[:, cs(q)] = applied
        sol[:, cs(q)] = degree
    for k in range(1, groups):
        for c in range(cap):
            named = tile_id(up(k), g, c)
            total = jnp.zeros((probes, TILE), jnp.float32)
            for q in range(tiles):
                total = total + jnp.where(named == q, 1.0, 0.0) * vec2[:, cs(q)]
            cvo2[k - 1, :, cs(c)] = total
    send_vectors(1)

    for j in range(tiles):
        rows = split_rows(vec2[:, cs(j)], False)
        mown[0 : 2 * probes, cs(j)] = rows
        mtile[j, 0 : 2 * probes] = rows
    two = 2 * probes

    @pl.loop(0, tiles)
    def _(i):
        acc[i, 0:two] = mxu(mown[0:two], kmat[0, i], NT)

    def merged(q):
        return merge_rows(acc[q, 0:two], probes, False)

    quad_local = jnp.zeros((probes, 1), jnp.float32)
    for q in range(tiles):
        quad_local = quad_local + jnp.sum(vec2[:, cs(q)] * merged(q), axis=1, keepdims=True)

    def band_again(block):
        vec_in(1, block).wait_recv()
        for j in range(tiles):
            mrem[0:two, cs(j)] = split_rows(vin2[block, :, cs(j)], False)
        hout2[block] = jnp.zeros((probes, cols), jnp.float32)

        @pl.loop(0, tiles)
        def _(i):
            value = kmat[1 + block, i]
            acc[i, 0:two] += mxu(mrem[0:two], value, NT)
            hout2[block] += merge_rows(mxu(mtile[i, 0:two], value, NN), probes, False)

        hand(1, block).start()

    def cross_again(k):
        cvec(1, k).wait_recv()
        for c in range(cap):
            mc[k - 1, 0:two, cs(c)] = split_rows(cvi2[k - 1, :, cs(c)], False)
        cho2[k - 1] = jnp.zeros((probes, cap * TILE), jnp.float32)

        @pl.loop(0, tiles)
        def _(i):
            value = kc[k - 1, i]
            acc[i, 0:two] += mxu(mc[k - 1, 0:two], value, NT)
            cho2[k - 1] += merge_rows(mxu(mtile[i, 0:two], value, NN), probes, False)

        chand(1, k).start()

    for block in range(2):
        @pl.when(has_block[block])
        def _():
            band_again(block)

    for k in range(1, groups):
        cross_again(k)

    parts = [jnp.zeros((probes, 1), jnp.float32) for _ in range(5)]
    for q in range(tiles):
        base, applied, degree = tgt[:, cs(q)], vec2[:, cs(q)], sol[:, cs(q)]
        terms = (base * base, base * applied, applied * applied, degree * applied * applied, applied * merged(q))
        parts = [old + jnp.sum(term, axis=1, keepdims=True) for old, term in zip(parts, terms)]
    quad = 2.0 * parts[4] - quad_local
    curved = noise_level * parts[2] + coupling_weight * (parts[3] - quad)
    lane = lax.broadcasted_iota(jnp.int32, (probes, 128), 1)
    message = jnp.zeros((probes, 128), jnp.float32)
    for index, part in enumerate((parts[0], parts[1], parts[2], curved)):
        message = message + jnp.where(lane == index, part, 0.0)
    red1o[...] = message

    def reduce_one(k):
        return remote(red1o, red1.at[k - 1], r1send.at[k - 1], r1recv.at[k - 1], {"group": up(k)})

    def reduce_two(k):
        return remote(red2o, red2.at[k - 1], r2send.at[k - 1], r2recv.at[k - 1], {"dev": lax.rem(d + k, devs)})

    for k in range(1, groups):
        reduce_one(k).start()
    for k in range(1, groups):
        reduce_one(k).wait_recv()
    for k in range(1, groups):
        message = message + red1[k - 1]
    red2o[...] = message
    for k in range(1, devs):
        reduce_two(k).start()

    wait_hands(1)
    sums = [merged(q) + hin2[0, :, cs(q)] + hin2[1, :, cs(q)] for q in range(tiles)]
    sums = gather_backs(1, sums)
    for q in range(tiles):
        applied, degree = vec2[:, cs(q)], sol[:, cs(q)]
        res[:, cs(q)] = noise_level * applied + coupling_weight * (degree * applied - sums[q])
    for k in range(1, devs):
        reduce_two(k).wait_recv()
    for k in range(1, devs):
        message = message + red2[k - 1]
    norm0, curv0, app_sq, app_curv = [
        jnp.sum(jnp.where(lane == index, message, 0.0), axis=1, keepdims=True) for index in range(4)
    ]
    step0 = norm0 / curv0
    norm1 = norm0 - 2.0 * step0 * curv0 + step0 * step0 * app_sq
    mix = 1.0 + norm1 / norm0
    curv1 = mix * mix * curv0 - 2.0 * mix * step0 * app_sq + step0 * step0 * app_curv
    step1 = norm1 / curv1
    for q in range(tiles):
        base, applied, twice = tgt[:, cs(q)], vec2[:, cs(q)], res[:, cs(q)]
        sol[:, cs(q)] = step0 * base + step1 * (mix * base - step0 * applied)
        res[:, cs(q)] = (base - step0 * applied) - step1 * (mix * applied - step0 * twice)

    for r in range(2):
        for which, cond in ((0, has_next), (1, has_far)):
            @pl.when(cond)
            def _():
                vec_copy(r, which).wait_send()
        for block in range(2):
            @pl.when(has_block[block])
            def _():
                hand(r, block).wait_send()
        for k in range(1, groups):
            cvec(r, k).wait_send()
            chand(r, k).wait_send()
    for k in range(1, groups):
        cpts(k).wait_send()
        reduce_one(k).wait_send()
    for k in range(1, devs):
        reduce_two(k).wait_send()

    @pl.when(has_far)
    def _():
        far_pts.wait_send()

    @pl.when(even)
    def _():
        mate_pts.wait_send()

    @pl.when(jnp.logical_and(odd, has_second))
    def _():
        forward_pts.wait_send()


def on_device(points, targets, partner_tiles):
    groups, devs, _, cap = partner_tiles.shape
    rows, features = points.shape
    tiles = rows // TILE
    probes = targets.shape[0]
    peers = groups - 1
    f32, bf16 = jnp.float32, jnp.bfloat16
    v = pltpu.VMEM
    dma = pltpu.SemaphoreType.DMA
    wide = cap * TILE
    two = 2 * probes
    scratch = [
        v((2, tiles, TILE, features), bf16),
        v((peers, cap, TILE, features), bf16),
        v((peers, cap, TILE, features), bf16),
        v((3, tiles, TILE, rows), bf16),
        v((peers, tiles, TILE, wide), bf16),
        v((tiles, TILE, 1), f32),
        v((two, rows), f32),
        v((2, two, rows), f32),
        v((peers, two, wide), f32),
        v((peers, two, wide), f32),
        v((probes, rows), f32),
        v((2, probes, rows), f32),
        v((peers, probes, wide), f32),
        v((peers, probes, wide), f32),
        v((2, two, rows), f32),
        v((2, two, rows), f32),
        v((peers, two, wide), f32),
        v((peers, two, wide), f32),
        v((2, probes, rows), f32),
        v((2, probes, rows), f32),
        v((peers, probes, wide), f32),
        v((peers, probes, wide), f32),
        v((2 * two, rows), bf16),
        v((tiles, 2 * two, TILE), bf16),
        v((2 * two, rows), bf16),
        v((peers, 2 * two, wide), bf16),
        v((tiles, 2 * two, TILE), f32),
        v((probes, 128), f32),
        v((peers, probes, 128), f32),
        v((probes, 128), f32),
        v((devs - 1, probes, 128), f32),
        dma((2,)), dma((2,)), dma((peers,)), dma((peers,)),
        dma((2, 2)), dma((2, 2)), dma((2, peers)), dma((2, peers)),
        dma((2, 2)), dma((2, 2)), dma((2, peers)), dma((2, peers)),
        dma((peers,)), dma((peers,)), dma((devs - 1,)), dma((devs - 1,)),
    ]
    pairs = rows * rows * 3 + rows * wide * peers
    return pl.pallas_call(
        functools.partial(kernel, groups, devs, cap, probes, tiles),
        out_shape=(jax.ShapeDtypeStruct(targets.shape, f32), jax.ShapeDtypeStruct(targets.shape, f32)),
        in_specs=[
            pl.BlockSpec(memory_space=pltpu.SMEM),
            pl.BlockSpec(memory_space=pltpu.VMEM),
            pl.BlockSpec(memory_space=pltpu.VMEM),
        ],
        out_specs=(pl.BlockSpec(memory_space=pltpu.VMEM), pl.BlockSpec(memory_space=pltpu.VMEM)),
        scratch_shapes=scratch,
        compiler_params=pltpu.CompilerParams(
            collective_id=0, has_side_effects=True, vmem_limit_bytes=56 * 1024 * 1024
        ),
        cost_estimate=pl.CostEstimate(flops=2 * features * pairs, bytes_accessed=rows * features * 2, transcendentals=pairs),
        name="graph_cg",
    )(partner_tiles.reshape(-1), points.reshape(tiles, TILE, features), targets)


def solution(mesh):
    return jax.shard_map(
        on_device,
        mesh=mesh,
        in_specs=(P(("group", "dev"), None), P(None, ("group", "dev")), P()),
        out_specs=(P(None, ("group", "dev")), P(None, ("group", "dev"))),
        check_vma=False,
    )
```

time: 396 us -> 119 us (0.30); the launches traced: 388 us -> 119 us
  matrix products: 152 us -> 0 us
  blocking collectives: 124 us -> 0 us
  Pallas kernels: 0 us -> 114 us
  starting transfers between devices: 54.2 us -> 0 us
  local copies, waits for them, and re-layouts: 28.9 us -> 4.44 us
  other arithmetic: 16.9 us -> 0 us
  loops' own time: 5.66 us -> 0 us
  waiting for transfers between devices: 5.5 us -> 0 us
    dot_general x23 -> x0, matrix products: 152 us -> none  [the longest x6 52.2 us: contract_last(): lax.dot_general(left_values, right_values, (((1,), (1,)), ((), ())), prec...]
    psum x3 -> x0, blocking collectives: 124 us -> none  [global_total(): return lax.psum(values, ('group', 'dev'))]
    pallas_call x0 -> x1, Pallas kernels: none -> 114 us  [on_device(): pl.pallas_call(functools.partial(kernel, groups, devs, cap, probes, tiles...]
    all_to_all x5 -> x0, starting transfers between devices: 28.8 us -> none  [the longest x4 23.1 us: trade_tiles(): lax.all_to_all(values, 'group', split_axis=1, concat_axis=1, tiled=True)]
    ppermute x10 -> x0, starting transfers between devices: 25.4 us -> none  [shifted(): lax.ppermute(value, axis, [(source, source + steps) for source in range(l...]
    dynamic_update_slice x8 -> x0, local copies, waits for them, and re-layouts: 10.2 us -> none  [cross_fill(): return lax.dynamic_update_index_in_dim(stored, blocks, slot_index, 0)]
    reduce_sum x9 -> x0, other arithmetic: 8.64 us -> none  [the longest x7 8.29 us: squares(): return jnp.sum(jnp.square(values.astype(jnp.float32)), axis=1)]
    another operation x9 -> x0, loops' own time: 5.66 us -> none  [the longest x1 5.5 us: on_device(): lax.fori_loop(0, slot_count, cross_fill, jnp.zeros((slot_count, row_count...]
  transfers between devices with their start and end apart: 15 -> 0, of which waited for: 1 -> 0; matrix products, arithmetic and copies ran while one was open for 36% -> 0% of each run, Pallas kernels for 0% -> 0%
where the time goes in v1:
time: 119 us
  Pallas kernels  114 us (96%)
  local copies, waits for them, and re-layouts  4.44 us (4%)
    pallas_call x1, Pallas kernels, on_device(): pl.pallas_call(functools.partial(kernel, groups, devs, cap, probes, tiles...  114 us
    unnamed x3, local copies, waits for them, and re-layouts  3.73 us

profile of v1, /device:TPU:0, one launch (start us, length us, event | category | flops | bytes accessed | tf_op | source)
XLA Modules:
  0.0 119.0 jit_solution(15780068580050461795)
XLA Ops:
  0.6 0.9 copy.5
  1.5 0.7 reshape.10.tab
  2.2 113.9 %graph_cg.1 = (f32[8,1536]{1,0:T(8,128)}, f32[8,1536]{1,0:T(8,128)}) custom-call(s32[256]{0:T(256)} %reshape.10.tab, bf16[6,256,512]{2,1,0:T(8,128)(2,1)} %bitcast.1, f32[8,1536]{1,0:T(8,128)} %tgt.1), custom_call_target="tpu_custom_call" | custom-call | flops 9663676416 | bytes 1572864 | tf_op jit(solution)/shard_map/graph_cg/pallas_call | solution.py:477
  116.1 1.4 %copy.8 = f32[8,1536]{1,0:T(8,128)} copy(f32[8,1536]{1,0:T(8,128)} %get-tuple-element.4) | data formatting | bytes 98304
  117.5 1.4 %copy.9 = f32[8,1536]{1,0:T(8,128)} copy(f32[8,1536]{1,0:T(8,128)} %get-tuple-element.5) | data formatting | bytes 98304

commit v2 on v1

--- a/solution.py
+++ b/solution.py
@@ -12,6 +12,7 @@
 length_scale = 3.9
 noise_level = 1.0
 coupling_weight = 0.5
+value_weight = coupling_weight * 4.0 / length_scale**5
 MESH = pl.DeviceIdType.MESH
 NT = (((1,), (1,)), ((), ()))
 NN = (((1,), (0,)), ((), ()))
@@ -37,10 +38,10 @@
 
 
 def kernel(groups, devs, cap, probes, tiles,
-           tab, pts, tgt, sol, res,
+           tab, pts, tgt, sol0, sol1, res0, res1,
            pin, outp, inp, kmat, kc, ncol, vec1, vin1, cvo1, cvi1, vec2, vin2, cvo2, cvi2,
            hout1, hin1, cho1, chi1, hout2, hin2, cho2, chi2,
-           mown, mtile, mrem, mc, acc, red1o, red1, red2o, red2,
+           mown, mtile, mrem, mc, acc, acc2, deg, red1o, red1, red2o, red2,
            psend, precv, cpsend, cprecv, vsend, vrecv, cvsend, cvrecv,
            hsend, hrecv, chsend, chrecv, r1send, r1recv, r2send, r2recv):
     g = lax.axis_index("group")
@@ -52,7 +53,7 @@
     cols = tiles * TILE
 
     def tile_id(owner, other, c):
-        return tab[((owner * devs + d) * groups + other) * cap + c]
+        return tab[owner, d, other, c]
 
     def up(k):
         return lax.rem(g + k, groups)
@@ -166,22 +167,44 @@
     def _():
         mate_pts.start()
 
-    def affinity(own, norm_col, other, norm_row):
-        inner = mxu(own, other, NT)
-        dist_sq = jnp.maximum(norm_col + norm_row - 2.0 * inner, 0.0)
-        scaled = dist_sq * lax.rsqrt(jnp.maximum(dist_sq, 1e-30)) * (1.0 / length_scale)
-        near = jnp.maximum(1.0 - scaled, 0.0)
-        near = near * near
-        return near * near * (4.0 * scaled + 1.0)
-
-    @pl.loop(0, tiles)
-    def _(i):
-        total = jnp.zeros((4 * probes, TILE), jnp.float32)
-        for j in range(tiles):
-            value = affinity(pts[i], ncol[i], pts[j], vec1[probes : probes + 1, cs(j)]).astype(jnp.bfloat16)
+    def doubled(i):
+        return pts[i] * jnp.asarray(-2.0, pts.dtype)
+
+    def affinity(inner, norm_col, norm_row):
+        dist_sq = jnp.maximum((norm_col + norm_row) + inner, 1e-30)
+        near = jnp.maximum(length_scale - dist_sq * lax.rsqrt(dist_sq), 0.0)
+        square = near * near
+        return square * square * (1.25 * length_scale - near)
+
+    def row_block(i, count, others, norm_row, finish):
+        own = doubled(i)
+        norm_col = jnp.broadcast_to(ncol[i], (TILE, TILE))
+        inner = mxu(own, others(0), NT)
+        for j in range(count):
+            ahead = mxu(own, others(j + 1), NT) if j + 1 < count else None
+            finish(j, affinity(inner, norm_col, norm_row(j)))
+            inner = ahead
+
+    fold = 2 if tiles % 2 == 0 else 1
+
+    def row_loop(body):
+        @pl.loop(0, tiles // fold)
+        def _(step):
+            for part in range(fold):
+                body(step * fold + part)
+
+    def own_rows(i):
+        total = [jnp.zeros((4 * probes, TILE), jnp.float32)]
+
+        def finish(j, value):
+            value = value.astype(jnp.bfloat16)
             kmat[0, i, :, cs(j)] = value
-            total = total + mxu(mown[:, cs(j)], value, NT)
-        acc[i] = total
+            total[0] = total[0] + mxu(mown[:, cs(j)], value, NT)
+
+        row_block(i, tiles, lambda j: pts[j], lambda j: vec1[probes : probes + 1, cs(j)], finish)
+        acc[i] = total[0]
+
+    row_loop(own_rows)
 
     def band(block):
         vec_in(0, block).wait_recv()
@@ -189,18 +212,19 @@
             mrem[:, cs(j)] = split_rows(vin1[block, 0:probes, cs(j)], True)
         hout1[block] = jnp.zeros((2 * probes, cols), jnp.float32)
 
-        @pl.loop(0, tiles)
-        def _(i):
-            total = acc[i]
-            for j in range(tiles):
-                value = affinity(
-                    pts[i], ncol[i], pin[block, j], vin1[block, probes : probes + 1, cs(j)]
-                ).astype(jnp.bfloat16)
+        def rows(i):
+            total = [acc[i]]
+
+            def finish(j, value):
+                value = value.astype(jnp.bfloat16)
                 kmat[1 + block, i, :, cs(j)] = value
-                total = total + mxu(mrem[:, cs(j)], value, NT)
+                total[0] = total[0] + mxu(mrem[:, cs(j)], value, NT)
                 hout1[block, :, cs(j)] += merge_rows(mxu(mtile[i], value, NN), probes, True)
-            acc[i] = total
-
+
+            row_block(i, tiles, lambda j: pin[block, j], lambda j: vin1[block, probes : probes + 1, cs(j)], finish)
+            acc[i] = total[0]
+
+        row_loop(rows)
         hand(0, block).start()
 
     def cross(k):
@@ -211,19 +235,19 @@
             mc[k - 1, :, cs(c)] = split_rows(cvi1[k - 1, 0:probes, cs(c)], True)
         cho1[k - 1] = jnp.zeros((2 * probes, cap * TILE), jnp.float32)
 
-        @pl.loop(0, tiles)
-        def _(i):
-            total = acc[i]
-            for c in range(cap):
-                value = affinity(
-                    pts[i], ncol[i], inp[k - 1, c], cvi1[k - 1, probes : probes + 1, cs(c)]
-                )
+        def rows(i):
+            total = [acc[i]]
+
+            def finish(c, value):
                 value = (value * live[c]).astype(jnp.bfloat16)
                 kc[k - 1, i, :, cs(c)] = value
-                total = total + mxu(mc[k - 1, :, cs(c)], value, NT)
+                total[0] = total[0] + mxu(mc[k - 1, :, cs(c)], value, NT)
                 cho1[k - 1, :, cs(c)] += merge_rows(mxu(mtile[i], value, NN), probes, True)
-            acc[i] = total
-
+
+            row_block(i, cap, lambda c: inp[k - 1, c], lambda c: cvi1[k - 1, probes : probes + 1, cs(c)], finish)
+            acc[i] = total[0]
+
+        row_loop(rows)
         chand(0, k).start()
 
     @pl.when(has_first)
@@ -264,7 +288,6 @@
             def _():
                 hand_in(r, slot).wait_recv()
 
-    incoming_ok = [jnp.where(has_next, 1.0, 0.0), jnp.where(has_far, 1.0, 0.0)]
     for slot, cond in ((0, has_next), (1, has_far)):
         @pl.when(jnp.logical_not(cond))
         def _():
@@ -277,9 +300,9 @@
     for q in range(tiles):
         base = tgt[:, cs(q)]
         degree = sums[q][probes : 2 * probes]
-        applied = noise_level * base + coupling_weight * (degree * base - sums[q][0:probes])
+        applied = noise_level * base + value_weight * (degree * base - sums[q][0:probes])
         vec2[:, cs(q)] = applied
-        sol[:, cs(q)] = degree
+        deg[:, cs(q)] = degree
     for k in range(1, groups):
         for c in range(cap):
             named = tile_id(up(k), g, c)
@@ -292,15 +315,15 @@
     for j in range(tiles):
         rows = split_rows(vec2[:, cs(j)], False)
         mown[0 : 2 * probes, cs(j)] = rows
-        mtile[j, 0 : 2 * probes] = rows
     two = 2 * probes
 
-    @pl.loop(0, tiles)
-    def _(i):
-        acc[i, 0:two] = mxu(mown[0:two], kmat[0, i], NT)
+    def whole(block):
+        return kmat[block].reshape(cols, cols)
+
+    acc2[...] = merge_rows(mxu(mown[0:two], whole(0), NT), probes, False)
 
     def merged(q):
-        return merge_rows(acc[q, 0:two], probes, False)
+        return acc2[:, cs(q)]
 
     quad_local = jnp.zeros((probes, 1), jnp.float32)
     for q in range(tiles):
@@ -310,28 +333,18 @@
         vec_in(1, block).wait_recv()
         for j in range(tiles):
             mrem[0:two, cs(j)] = split_rows(vin2[block, :, cs(j)], False)
-        hout2[block] = jnp.zeros((probes, cols), jnp.float32)
-
-        @pl.loop(0, tiles)
-        def _(i):
-            value = kmat[1 + block, i]
-            acc[i, 0:two] += mxu(mrem[0:two], value, NT)
-            hout2[block] += merge_rows(mxu(mtile[i, 0:two], value, NN), probes, False)
-
+        value = whole(1 + block)
+        hout2[block] = merge_rows(mxu(mown[0:two], value, NN), probes, False)
+        acc2[...] += merge_rows(mxu(mrem[0:two], value, NT), probes, False)
         hand(1, block).start()
 
     def cross_again(k):
         cvec(1, k).wait_recv()
         for c in range(cap):
             mc[k - 1, 0:two, cs(c)] = split_rows(cvi2[k - 1, :, cs(c)], False)
-        cho2[k - 1] = jnp.zeros((probes, cap * TILE), jnp.float32)
-
-        @pl.loop(0, tiles)
-        def _(i):
-            value = kc[k - 1, i]
-            acc[i, 0:two] += mxu(mc[k - 1, 0:two], value, NT)
-            cho2[k - 1] += merge_rows(mxu(mtile[i, 0:two], value, NN), probes, False)
-
+        value = kc[k - 1].reshape(cols, cap * TILE)
+        cho2[k - 1] = merge_rows(mxu(mown[0:two], value, NN), probes, False)
+        acc2[...] += merge_rows(mxu(mc[k - 1, 0:two], value, NT), probes, False)
         chand(1, k).start()
 
     for block in range(2):
@@ -344,11 +357,11 @@
 
     parts = [jnp.zeros((probes, 1), jnp.float32) for _ in range(5)]
     for q in range(tiles):
-        base, applied, degree = tgt[:, cs(q)], vec2[:, cs(q)], sol[:, cs(q)]
+        base, applied, degree = tgt[:, cs(q)], vec2[:, cs(q)], deg[:, cs(q)]
         terms = (base * base, base * applied, applied * applied, degree * applied * applied, applied * merged(q))
         parts = [old + jnp.sum(term, axis=1, keepdims=True) for old, term in zip(parts, terms)]
     quad = 2.0 * parts[4] - quad_local
-    curved = noise_level * parts[2] + coupling_weight * (parts[3] - quad)
+    curved = noise_level * parts[2] + value_weight * (parts[3] - quad)
     lane = lax.broadcasted_iota(jnp.int32, (probes, 128), 1)
     message = jnp.zeros((probes, 128), jnp.float32)
     for index, part in enumerate((parts[0], parts[1], parts[2], curved)):
@@ -375,8 +388,8 @@
     sums = [merged(q) + hin2[0, :, cs(q)] + hin2[1, :, cs(q)] for q in range(tiles)]
     sums = gather_backs(1, sums)
     for q in range(tiles):
-        applied, degree = vec2[:, cs(q)], sol[:, cs(q)]
-        res[:, cs(q)] = noise_level * applied + coupling_weight * (degree * applied - sums[q])
+        applied, degree = vec2[:, cs(q)], deg[:, cs(q)]
+        res1[:, cs(q)] = noise_level * applied + value_weight * (degree * applied - sums[q])
     for k in range(1, devs):
         reduce_two(k).wait_recv()
     for k in range(1, devs):
@@ -390,9 +403,11 @@
     curv1 = mix * mix * curv0 - 2.0 * mix * step0 * app_sq + step0 * step0 * app_curv
     step1 = norm1 / curv1
     for q in range(tiles):
-        base, applied, twice = tgt[:, cs(q)], vec2[:, cs(q)], res[:, cs(q)]
-        sol[:, cs(q)] = step0 * base + step1 * (mix * base - step0 * applied)
-        res[:, cs(q)] = (base - step0 * applied) - step1 * (mix * applied - step0 * twice)
+        base, applied, twice = tgt[:, cs(q)], vec2[:, cs(q)], res1[:, cs(q)]
+        sol0[:, cs(q)] = step0 * base
+        sol1[:, cs(q)] = step1 * (mix * base - step0 * applied)
+        res0[:, cs(q)] = base - step0 * applied
+        res1[:, cs(q)] = step1 * (mix * applied - step0 * twice)
 
     for r in range(2):
         for which, cond in ((0, has_next), (1, has_far)):
@@ -464,6 +479,8 @@
         v((2 * two, rows), bf16),
         v((peers, 2 * two, wide), bf16),
         v((tiles, 2 * two, TILE), f32),
+        v((probes, rows), f32),
+        v((probes, rows), f32),
         v((probes, 128), f32),
         v((peers, probes, 128), f32),
         v((probes, 128), f32),
@@ -474,22 +491,23 @@
         dma((peers,)), dma((peers,)), dma((devs - 1,)), dma((devs - 1,)),
     ]
     pairs = rows * rows * 3 + rows * wide * peers
-    return pl.pallas_call(
+    sol0, sol1, res0, res1 = pl.pallas_call(
         functools.partial(kernel, groups, devs, cap, probes, tiles),
-        out_shape=(jax.ShapeDtypeStruct(targets.shape, f32), jax.ShapeDtypeStruct(targets.shape, f32)),
+        out_shape=(jax.ShapeDtypeStruct(targets.shape, f32),) * 4,
         in_specs=[
             pl.BlockSpec(memory_space=pltpu.SMEM),
             pl.BlockSpec(memory_space=pltpu.VMEM),
             pl.BlockSpec(memory_space=pltpu.VMEM),
         ],
-        out_specs=(pl.BlockSpec(memory_space=pltpu.VMEM), pl.BlockSpec(memory_space=pltpu.VMEM)),
+        out_specs=(pl.BlockSpec(memory_space=pltpu.VMEM),) * 4,
         scratch_shapes=scratch,
         compiler_params=pltpu.CompilerParams(
             collective_id=0, has_side_effects=True, vmem_limit_bytes=56 * 1024 * 1024
         ),
         cost_estimate=pl.CostEstimate(flops=2 * features * pairs, bytes_accessed=rows * features * 2, transcendentals=pairs),
         name="graph_cg",
-    )(partner_tiles.reshape(-1), points.reshape(tiles, TILE, features), targets)
+    )(partner_tiles, points.reshape(tiles, TILE, features), targets)
+    return (sol0 + sol1, res0 - res1)
 
 
 def solution(mesh):

time: 119 us -> 98.3 us (0.83)
  Pallas kernels: 114 us -> 92.9 us
  local copies, waits for them, and re-layouts: 4.44 us -> 1.5 us
  other arithmetic: 0 us -> 2.9 us
    pallas_call x1, Pallas kernels: 114 us -> 92.9 us  [on_device(): pl.pallas_call(functools.partial(kernel, groups, devs, cap, probes, tiles...]
    unnamed x3 -> x1, local copies, waits for them, and re-layouts: 3.73 us -> 1.5 us
    add x0 -> x1, other arithmetic: none -> 1.45 us  [on_device(): return (sol0 + sol1, res0 - res1)]
    sub x0 -> x1, other arithmetic: none -> 1.45 us  [on_device(): return (sol0 + sol1, res0 - res1)]
where the time goes in v2:
time: 98.3 us; the launch traced here: 97.9 us
  Pallas kernels  92.9 us (95%)
  other arithmetic  2.9 us (3%)
  local copies, waits for them, and re-layouts  1.5 us (2%)
    pallas_call x1, Pallas kernels, on_device(): pl.pallas_call(functools.partial(kernel, groups, devs, cap, probes, tiles...  92.9 us

profile of v2, /device:TPU:0, one launch (start us, length us, event | category | flops | bytes accessed | tf_op | source)
XLA Modules:
  0.0 97.9 jit_solution(6351026908366587423)
XLA Ops:
  0.6 1.5 %copy.5.tab = s32[4,8,4,2]{3,2,1,0:T(4,128)} copy(s32[4,8,4,2]{1,3,2,0:T(2,128)} %param.5) | data formatting | bytes 2048 | tf_op args[2]
  2.1 92.9 %graph_cg.1 = (f32[8,1536]{1,0:T(8,128)}, f32[8,1536]{1,0:T(8,128)}, f32[8,1536]{1,0:T(8,128)}, f32[8,1536]{1,0:T(8,128)}) custom-call(s32[4,8,4,2]{3,2,1,0:T(4,128)} %copy.5.tab, bf16[6,256,512]{2,1,0:T(8,128)(2,1)} %bitcast.1, f32[8,1536]{1,0:T(8,128)} %tgt.1), custom_call_target="tpu_custom_call" | custom-call | flops 9663676416 | bytes 1572864 | tf_op jit(solution)/shard_map/graph_cg/pallas_call | solution.py:494
  95.0 1.4 %add.3 = f32[8,1536]{1,0:T(8,128)} add(f32[8,1536]{1,0:T(8,128)} %get-tuple-element.6, f32[8,1536]{1,0:T(8,128)} %get-tuple-element.7) | non-fusion elementwise | flops 12288 | bytes 147456 | tf_op jit(solution)/shard_map/add | solution.py:510
  96.5 1.4 %sub.3 = f32[8,1536]{1,0:T(8,128)} subtract(f32[8,1536]{1,0:T(8,128)} %get-tuple-element.8, f32[8,1536]{1,0:T(8,128)} %get-tuple-element.9) | non-fusion elementwise | flops 12288 | bytes 147456 | tf_op jit(solution)/shard_map/sub | solution.py:510

commit v3 on v2

--- a/solution.py
+++ b/solution.py
@@ -38,8 +38,8 @@
 
 
 def kernel(groups, devs, cap, probes, tiles,
-           tab, pts, tgt, sol0, sol1, res0, res1,
-           pin, outp, inp, kmat, kc, ncol, vec1, vin1, cvo1, cvi1, vec2, vin2, cvo2, cvi2,
+           tab, pts, tgt, sol0, sol1, res1,
+           pin, outp, inp, kmat, kc, ncol, twin, vec1, vin1, cvo1, cvi1, vec2, vin2, cvo2, cvi2,
            hout1, hin1, cho1, chi1, hout2, hin2, cho2, chi2,
            mown, mtile, mrem, mc, acc, acc2, deg, red1o, red1, red2o, red2,
            psend, precv, cpsend, cprecv, vsend, vrecv, cvsend, cvrecv,
@@ -53,7 +53,7 @@
     cols = tiles * TILE
 
     def tile_id(owner, other, c):
-        return tab[owner, d, other, c]
+        return tab[owner, other, c, d]
 
     def up(k):
         return lax.rem(g + k, groups)
@@ -63,10 +63,17 @@
 
     def cs(j):
         return slice(j * TILE, (j + 1) * TILE)
+
+    barrier = pltpu.get_barrier_semaphore()
+    for k in range(1, groups):
+        pl.semaphore_signal(barrier, inc=1, device_id={"group": up(k)}, device_id_type=MESH)
+    for k in range(1, devs):
+        pl.semaphore_signal(barrier, inc=1, device_id={"dev": lax.rem(d + k, devs)}, device_id_type=MESH)
 
     @pl.loop(0, tiles)
     def _(i):
         wide = pts[i].astype(jnp.float32)
+        twin[i] = pts[i] * jnp.asarray(-2.0, pts.dtype)
         ncol[i] = jnp.sum(wide * wide, axis=1, keepdims=True)
 
     for j in range(tiles):
@@ -90,11 +97,6 @@
                 total = total + jnp.where(named == q, 1.0, 0.0) * vec1[:, cs(q)]
             cvo1[k - 1, :, cs(c)] = total
 
-    barrier = pltpu.get_barrier_semaphore()
-    for k in range(1, groups):
-        pl.semaphore_signal(barrier, inc=1, device_id={"group": up(k)}, device_id_type=MESH)
-    for k in range(1, devs):
-        pl.semaphore_signal(barrier, inc=1, device_id={"dev": lax.rem(d + k, devs)}, device_id_type=MESH)
     pl.semaphore_wait(barrier, groups + devs - 2)
 
     def remote(src, dst, ssem, rsem, where):
@@ -143,9 +145,24 @@
     def cpts(k):
         return remote(outp.at[k - 1], inp.at[k - 1], cpsend.at[k - 1], cprecv.at[k - 1], {"group": up(k)})
 
-    far_pts = remote(pts, pin.at[par], psend.at[1], precv.at[par], {"dev": far})
-    mate_pts = remote(pts, pin.at[0], psend.at[0], precv.at[0], {"dev": nxt})
-    forward_pts = remote(pin.at[1], pin.at[1], psend.at[0], precv.at[1], {"dev": jnp.maximum(d - 1, 0)})
+    fold = 2 if tiles % 2 == 0 else 1
+    chunks = tiles // fold
+
+    def piece(s):
+        return pl.ds(s * fold, fold)
+
+    def far_pts(s):
+        return remote(pts.at[piece(s)], pin.at[par, piece(s)], psend.at[1, s], precv.at[par, s], {"dev": far})
+
+    def mate_pts(s):
+        return remote(pts.at[piece(s)], pin.at[0, piece(s)], psend.at[0, s], precv.at[0, s], {"dev": nxt})
+
+    def forward_pts(s):
+        return remote(pin.at[1, piece(s)], pin.at[1, piece(s)], psend.at[0, s], precv.at[1, s],
+                      {"dev": jnp.maximum(d - 1, 0)})
+
+    def pts_in(block, s):
+        return remote(pts.at[piece(s)], pin.at[block, piece(s)], psend.at[0, s], precv.at[block, s], {"dev": nxt})
 
     def send_vectors(r):
         for which, cond in ((0, has_next), (1, has_far)):
@@ -156,19 +173,20 @@
             cvec(r, k).start()
 
     send_vectors(0)
-    for k in range(1, groups):
+    cpts(1).start()
+
+    @pl.when(even)
+    def _():
+        for s in range(chunks):
+            mate_pts(s).start()
+
+    @pl.when(has_far)
+    def _():
+        for s in range(chunks):
+            far_pts(s).start()
+
+    for k in range(2, groups):
         cpts(k).start()
-
-    @pl.when(has_far)
-    def _():
-        far_pts.start()
-
-    @pl.when(even)
-    def _():
-        mate_pts.start()
-
-    def doubled(i):
-        return pts[i] * jnp.asarray(-2.0, pts.dtype)
 
     def affinity(inner, norm_col, norm_row):
         dist_sq = jnp.maximum((norm_col + norm_row) + inner, 1e-30)
@@ -177,7 +195,7 @@
         return square * square * (1.25 * length_scale - near)
 
     def row_block(i, count, others, norm_row, finish):
-        own = doubled(i)
+        own = twin[i]
         norm_col = jnp.broadcast_to(ncol[i], (TILE, TILE))
         inner = mxu(own, others(0), NT)
         for j in range(count):
@@ -185,13 +203,11 @@
             finish(j, affinity(inner, norm_col, norm_row(j)))
             inner = ahead
 
-    fold = 2 if tiles % 2 == 0 else 1
-
     def row_loop(body):
         @pl.loop(0, tiles // fold)
         def _(step):
-            for part in range(fold):
-                body(step * fold + part)
+            for inner in range(fold):
+                body(step * fold + inner)
 
     def own_rows(i):
         total = [jnp.zeros((4 * probes, TILE), jnp.float32)]
@@ -208,23 +224,33 @@
 
     def band(block):
         vec_in(0, block).wait_recv()
-        for j in range(tiles):
-            mrem[:, cs(j)] = split_rows(vin1[block, 0:probes, cs(j)], True)
-        hout1[block] = jnp.zeros((2 * probes, cols), jnp.float32)
-
-        def rows(i):
-            total = [acc[i]]
-
-            def finish(j, value):
-                value = value.astype(jnp.bfloat16)
-                kmat[1 + block, i, :, cs(j)] = value
-                total[0] = total[0] + mxu(mrem[:, cs(j)], value, NT)
-                hout1[block, :, cs(j)] += merge_rows(mxu(mtile[i], value, NN), probes, True)
-
-            row_block(i, tiles, lambda j: pin[block, j], lambda j: vin1[block, probes : probes + 1, cs(j)], finish)
-            acc[i] = total[0]
-
-        row_loop(rows)
+
+        def column(j):
+            span = pl.ds(pl.multiple_of(j * TILE, TILE), TILE)
+            theirs = split_rows(vin1[block, 0:probes, span], True)
+            norm_row = vin1[block, probes : probes + 1, span]
+            total = jnp.zeros((4 * probes, TILE), jnp.float32)
+            inner = mxu(twin[0], pin[block, j], NT)
+            for i in range(tiles):
+                ahead = mxu(twin[i + 1], pin[block, j], NT) if i + 1 < tiles else None
+                value = affinity(inner, ncol[i], norm_row).astype(jnp.bfloat16)
+                kmat[1 + block, i, :, span] = value
+                acc[i] += mxu(theirs, value, NT)
+                total = total + mxu(mtile[i], value, NN)
+                inner = ahead
+            hout1[block, :, span] = merge_rows(total, probes, True)
+
+        @pl.loop(0, chunks)
+        def _(s):
+            pts_in(block, s).wait_recv()
+            if block == 1:
+                @pl.when(odd)
+                def _():
+                    forward_pts(s).start()
+
+            for inner in range(fold):
+                column(s * fold + inner)
+
         hand(0, block).start()
 
     def cross(k):
@@ -250,21 +276,18 @@
         row_loop(rows)
         chand(0, k).start()
 
-    @pl.when(has_first)
-    def _():
-        remote(pts, pin.at[0], psend.at[0], precv.at[0], {"dev": nxt}).wait_recv()
+    @pl.when(odd)
+    def _():
         band(0)
 
     cross(1)
 
+    @pl.when(jnp.logical_and(even, has_first))
+    def _():
+        band(0)
+
     @pl.when(has_second)
     def _():
-        remote(pts, pin.at[1], psend.at[0], precv.at[1], {"dev": nxt}).wait_recv()
-
-        @pl.when(odd)
-        def _():
-            forward_pts.start()
-
         band(1)
 
     for k in range(2, groups):
@@ -406,8 +429,8 @@
         base, applied, twice = tgt[:, cs(q)], vec2[:, cs(q)], res1[:, cs(q)]
         sol0[:, cs(q)] = step0 * base
         sol1[:, cs(q)] = step1 * (mix * base - step0 * applied)
-        res0[:, cs(q)] = base - step0 * applied
-        res1[:, cs(q)] = step1 * (mix * applied - step0 * twice)
+        left = (base - step0 * applied) - step1 * (mix * applied - step0 * twice)
+        res1[:, cs(q)] = left - step0 * base
 
     for r in range(2):
         for which, cond in ((0, has_next), (1, has_far)):
@@ -429,15 +452,18 @@
 
     @pl.when(has_far)
     def _():
-        far_pts.wait_send()
+        for s in range(chunks):
+            far_pts(s).wait_send()
 
     @pl.when(even)
     def _():
-        mate_pts.wait_send()
+        for s in range(chunks):
+            mate_pts(s).wait_send()
 
     @pl.when(jnp.logical_and(odd, has_second))
     def _():
-        forward_pts.wait_send()
+        for s in range(chunks):
+            forward_pts(s).wait_send()
 
 
 def on_device(points, targets, partner_tiles):
@@ -458,6 +484,7 @@
         v((3, tiles, TILE, rows), bf16),
         v((peers, tiles, TILE, wide), bf16),
         v((tiles, TILE, 1), f32),
+        v((tiles, TILE, features), bf16),
         v((two, rows), f32),
         v((2, two, rows), f32),
         v((peers, two, wide), f32),
@@ -485,29 +512,29 @@
         v((peers, probes, 128), f32),
         v((probes, 128), f32),
         v((devs - 1, probes, 128), f32),
-        dma((2,)), dma((2,)), dma((peers,)), dma((peers,)),
+        dma((2, tiles)), dma((2, tiles)), dma((peers,)), dma((peers,)),
         dma((2, 2)), dma((2, 2)), dma((2, peers)), dma((2, peers)),
         dma((2, 2)), dma((2, 2)), dma((2, peers)), dma((2, peers)),
         dma((peers,)), dma((peers,)), dma((devs - 1,)), dma((devs - 1,)),
     ]
     pairs = rows * rows * 3 + rows * wide * peers
-    sol0, sol1, res0, res1 = pl.pallas_call(
+    sol0, sol1, res1 = pl.pallas_call(
         functools.partial(kernel, groups, devs, cap, probes, tiles),
-        out_shape=(jax.ShapeDtypeStruct(targets.shape, f32),) * 4,
+        out_shape=(jax.ShapeDtypeStruct(targets.shape, f32),) * 3,
         in_specs=[
             pl.BlockSpec(memory_space=pltpu.SMEM),
             pl.BlockSpec(memory_space=pltpu.VMEM),
             pl.BlockSpec(memory_space=pltpu.VMEM),
         ],
-        out_specs=(pl.BlockSpec(memory_space=pltpu.VMEM),) * 4,
+        out_specs=(pl.BlockSpec(memory_space=pltpu.VMEM),) * 3,
         scratch_shapes=scratch,
         compiler_params=pltpu.CompilerParams(
             collective_id=0, has_side_effects=True, vmem_limit_bytes=56 * 1024 * 1024
         ),
         cost_estimate=pl.CostEstimate(flops=2 * features * pairs, bytes_accessed=rows * features * 2, transcendentals=pairs),
         name="graph_cg",
-    )(partner_tiles, points.reshape(tiles, TILE, features), targets)
-    return (sol0 + sol1, res0 - res1)
+    )(jnp.transpose(partner_tiles, (0, 2, 3, 1)), points.reshape(tiles, TILE, features), targets)
+    return (sol0 + sol1, sol0 + res1)
 
 
 def solution(mesh):

time: 98.3 us -> 97.2 us (0.989)
  Pallas kernels: 92.9 us -> 94.8 us
  local copies, waits for them, and re-layouts: 1.5 us -> 0 us
  other arithmetic: 2.9 us -> 1.49 us
    pallas_call x1, Pallas kernels: 92.9 us -> 94.8 us  [on_device(): pl.pallas_call(functools.partial(kernel, groups, devs, cap, probes, tiles...]
    unnamed x1 -> x0, local copies, waits for them, and re-layouts: 1.5 us -> none
    sub x1 -> x0, other arithmetic: 1.45 us -> none  [on_device(): return (sol0 + sol1, res0 - res1)]
where the time goes in v3:
time: 97.2 us; the launch traced here: 97 us
  Pallas kernels  94.8 us (98%)
  other arithmetic  1.49 us (2%)
    pallas_call x1, Pallas kernels, on_device(): pl.pallas_call(functools.partial(kernel, groups, devs, cap, probes, tiles...  94.8 us

profile of v3, /device:TPU:0, one launch (start us, length us, event | category | flops | bytes accessed | tf_op | source)
XLA Modules:
  0.0 97.0 jit_solution(11241637915173628696)
XLA Ops:
  0.6 94.8 %graph_cg.1 = (f32[8,1536]{1,0:T(8,128)}, f32[8,1536]{1,0:T(8,128)}, f32[8,1536]{1,0:T(8,128)}) custom-call(s32[4,4,2,8]{3,2,1,0:T(2,128)} %bitcast.3, bf16[6,256,512]{2,1,0:T(8,128)(2,1)} %bitcast.2, f32[8,1536]{1,0:T(8,128)} %tgt.1), custom_call_target="tpu_custom_call" | custom-call | flops 9663676416 | bytes 1572864 | tf_op jit(solution)/shard_map/graph_cg/pallas_call | solution.py:521
  95.5 1.5 %fusion = (f32[8,1536]{1,0:T(8,128)}, f32[8,1536]{1,0:T(8,128)}) fusion(f32[8,1536]{1,0:T(8,128)} %get-tuple-element.5, f32[8,1536]{1,0:T(8,128)} %get-tuple-element.7, f32[8,1536]{1,0:T(8,128)} %get-tuple-element.6), kind=kLoop, calls=%fused_computation | loop fusion | flops 24576 | bytes 245760 | tf_op jit(solution)/shard_map/add | solution.py:537

commit v4 on v3

--- a/solution.py
+++ b/solution.py
@@ -13,6 +13,7 @@
 noise_level = 1.0
 coupling_weight = 0.5
 value_weight = coupling_weight * 4.0 / length_scale**5
+PIECE = 32
 MESH = pl.DeviceIdType.MESH
 NT = (((1,), (1,)), ((), ()))
 NN = (((1,), (0,)), ((), ()))
@@ -39,9 +40,9 @@
 
 def kernel(groups, devs, cap, probes, tiles,
            tab, pts, tgt, sol0, sol1, res1,
-           pin, outp, inp, kmat, kc, ncol, twin, vec1, vin1, cvo1, cvi1, vec2, vin2, cvo2, cvi2,
+           pin, outp, inp, kmat, kc, ncol, twin, grama, gramb, vec1, vin1, cvo1, cvi1, vec2, vin2, cvo2, cvi2,
            hout1, hin1, cho1, chi1, hout2, hin2, cho2, chi2,
-           mown, mtile, mrem, mc, acc, acc2, deg, red1o, red1, red2o, red2,
+           mown, mrem, mc, acc, acc2, deg, red1o, red1, red2o, red2,
            psend, precv, cpsend, cprecv, vsend, vrecv, cvsend, cvrecv,
            hsend, hrecv, chsend, chrecv, r1send, r1recv, r2send, r2recv):
     g = lax.axis_index("group")
@@ -87,7 +88,6 @@
         vec1[probes : 2 * probes, cs(j)] = sums[0:probes]
         rows = split_rows(tgt[:, cs(j)], True)
         mown[:, cs(j)] = rows
-        mtile[j] = rows
     for k in range(1, groups):
         for c in range(cap):
             named = tile_id(up(k), g, c)
@@ -194,51 +194,44 @@
         square = near * near
         return square * square * (1.25 * length_scale - near)
 
-    def row_block(i, count, others, norm_row, finish):
-        own = twin[i]
-        norm_col = jnp.broadcast_to(ncol[i], (TILE, TILE))
-        inner = mxu(own, others(0), NT)
-        for j in range(count):
-            ahead = mxu(own, others(j + 1), NT) if j + 1 < count else None
-            finish(j, affinity(inner, norm_col, norm_row(j)))
-            inner = ahead
-
-    def row_loop(body):
-        @pl.loop(0, tiles // fold)
-        def _(step):
-            for inner in range(fold):
-                body(step * fold + inner)
-
-    def own_rows(i):
-        total = [jnp.zeros((4 * probes, TILE), jnp.float32)]
-
-        def finish(j, value):
-            value = value.astype(jnp.bfloat16)
-            kmat[0, i, :, cs(j)] = value
-            total[0] = total[0] + mxu(mown[:, cs(j)], value, NT)
-
-        row_block(i, tiles, lambda j: pts[j], lambda j: vec1[probes : probes + 1, cs(j)], finish)
-        acc[i] = total[0]
-
-    row_loop(own_rows)
+    def panels(other, theirs, norm_row, scale, put, get):
+        buffers = (grama, gramb)
+        width = norm_row.shape[1]
+        total = jnp.zeros((4 * probes, width), jnp.float32)
+        buffers[0][:, 0:width] = mxu(twin[0], other(), NT)
+        for i in range(tiles):
+            if i + 1 < tiles:
+                buffers[(i + 1) % 2][:, 0:width] = mxu(twin[i + 1], other(), NT)
+            for low in range(0, TILE, PIECE):
+                rows = slice(low, low + PIECE)
+                value = affinity(buffers[i % 2][rows, 0:width], ncol[i, rows], norm_row)
+                if scale is not None:
+                    value = value * scale
+                put(i, rows, value.astype(jnp.bfloat16))
+            acc[:, cs(i)] += mxu(theirs, get(i), NT)
+            total = total + mxu(mown[:, cs(i)], get(i), NN)
+        return total
+
+    def chunk_span(s):
+        width = fold * TILE
+        return pl.ds(pl.multiple_of(s * width, width), width)
+
+    def block_panels(block, s, other, theirs, norm_row):
+        def put(i, rows, value):
+            kmat[block, s, i, rows] = value
+
+        return panels(other, theirs, norm_row, None, put, lambda i: kmat[block, s, i])
+
+    acc[...] = jnp.zeros_like(acc)
+
+    @pl.loop(0, chunks)
+    def _(s):
+        span = chunk_span(s)
+        block_panels(0, s, lambda: pts[piece(s)].reshape(fold * TILE, pts.shape[2]),
+                     mown[:, span], vec1[probes : probes + 1, span])
 
     def band(block):
         vec_in(0, block).wait_recv()
-
-        def column(j):
-            span = pl.ds(pl.multiple_of(j * TILE, TILE), TILE)
-            theirs = split_rows(vin1[block, 0:probes, span], True)
-            norm_row = vin1[block, probes : probes + 1, span]
-            total = jnp.zeros((4 * probes, TILE), jnp.float32)
-            inner = mxu(twin[0], pin[block, j], NT)
-            for i in range(tiles):
-                ahead = mxu(twin[i + 1], pin[block, j], NT) if i + 1 < tiles else None
-                value = affinity(inner, ncol[i], norm_row).astype(jnp.bfloat16)
-                kmat[1 + block, i, :, span] = value
-                acc[i] += mxu(theirs, value, NT)
-                total = total + mxu(mtile[i], value, NN)
-                inner = ahead
-            hout1[block, :, span] = merge_rows(total, probes, True)
 
         @pl.loop(0, chunks)
         def _(s):
@@ -248,32 +241,30 @@
                 def _():
                     forward_pts(s).start()
 
-            for inner in range(fold):
-                column(s * fold + inner)
+            span = chunk_span(s)
+            theirs = split_rows(vin1[block, 0:probes, span], True)
+            total = block_panels(1 + block, s, lambda: pin[block, piece(s)].reshape(fold * TILE, pts.shape[2]),
+                                 theirs, vin1[block, probes : probes + 1, span])
+            hout1[block, :, span] = merge_rows(total, probes, True)
 
         hand(0, block).start()
 
     def cross(k):
         cvec(0, k).wait_recv()
         cpts(k).wait_recv()
-        live = [jnp.where(tile_id(g, down(k), c) >= 0, 1.0, 0.0) for c in range(cap)]
+        wide = cap * TILE
+        lane_tile = lax.broadcasted_iota(jnp.int32, (1, wide), 1) // TILE
+        live = jnp.zeros((1, wide), jnp.float32)
         for c in range(cap):
-            mc[k - 1, :, cs(c)] = split_rows(cvi1[k - 1, 0:probes, cs(c)], True)
-        cho1[k - 1] = jnp.zeros((2 * probes, cap * TILE), jnp.float32)
-
-        def rows(i):
-            total = [acc[i]]
-
-            def finish(c, value):
-                value = (value * live[c]).astype(jnp.bfloat16)
-                kc[k - 1, i, :, cs(c)] = value
-                total[0] = total[0] + mxu(mc[k - 1, :, cs(c)], value, NT)
-                cho1[k - 1, :, cs(c)] += merge_rows(mxu(mtile[i], value, NN), probes, True)
-
-            row_block(i, cap, lambda c: inp[k - 1, c], lambda c: cvi1[k - 1, probes : probes + 1, cs(c)], finish)
-            acc[i] = total[0]
-
-        row_loop(rows)
+            live = live + jnp.where(tile_id(g, down(k), c) >= 0, 1.0, 0.0) * jnp.where(lane_tile == c, 1.0, 0.0)
+        theirs = split_rows(cvi1[k - 1, 0:probes], True)
+
+        def put(i, rows, value):
+            kc[k - 1, i, rows] = value
+
+        total = panels(lambda: inp[k - 1].reshape(wide, pts.shape[2]), theirs,
+                       cvi1[k - 1, probes : probes + 1], live, put, lambda i: kc[k - 1, i])
+        cho1[k - 1] = merge_rows(total, probes, True)
         chand(0, k).start()
 
     @pl.when(odd)
@@ -318,7 +309,7 @@
             hin2[slot] = jnp.zeros((probes, cols), jnp.float32)
 
     wait_hands(0)
-    sums = [merge_rows(acc[q], probes, True) + hin1[0, :, cs(q)] + hin1[1, :, cs(q)] for q in range(tiles)]
+    sums = [merge_rows(acc[:, cs(q)], probes, True) + hin1[0, :, cs(q)] + hin1[1, :, cs(q)] for q in range(tiles)]
     sums = gather_backs(0, sums)
     for q in range(tiles):
         base = tgt[:, cs(q)]
@@ -340,10 +331,16 @@
         mown[0 : 2 * probes, cs(j)] = rows
     two = 2 * probes
 
-    def whole(block):
-        return kmat[block].reshape(cols, cols)
-
-    acc2[...] = merge_rows(mxu(mown[0:two], whole(0), NT), probes, False)
+    def span_of(s):
+        return slice(s * fold * TILE, (s + 1) * fold * TILE)
+
+    def whole(block, s):
+        return kmat[block, s].reshape(cols, fold * TILE)
+
+    def own_sums(rows, block):
+        return sum(merge_rows(mxu(rows[0:two, span_of(s)], whole(block, s), NT), probes, False) for s in range(chunks))
+
+    acc2[...] = own_sums(mown, 0)
 
     def merged(q):
         return acc2[:, cs(q)]
@@ -356,10 +353,10 @@
         vec_in(1, block).wait_recv()
         for j in range(tiles):
             mrem[0:two, cs(j)] = split_rows(vin2[block, :, cs(j)], False)
-        value = whole(1 + block)
-        hout2[block] = merge_rows(mxu(mown[0:two], value, NN), probes, False)
-        acc2[...] += merge_rows(mxu(mrem[0:two], value, NT), probes, False)
+        for s in range(chunks):
+            hout2[block, :, span_of(s)] = merge_rows(mxu(mown[0:two], whole(1 + block, s), NN), probes, False)
         hand(1, block).start()
+        acc2[...] += own_sums(mrem, 1 + block)
 
     def cross_again(k):
         cvec(1, k).wait_recv()
@@ -477,14 +474,18 @@
     dma = pltpu.SemaphoreType.DMA
     wide = cap * TILE
     two = 2 * probes
+    fold = 2 if tiles % 2 == 0 else 1
+    span = max(fold, cap) * TILE
     scratch = [
         v((2, tiles, TILE, features), bf16),
         v((peers, cap, TILE, features), bf16),
         v((peers, cap, TILE, features), bf16),
-        v((3, tiles, TILE, rows), bf16),
+        v((3, tiles // fold, tiles, TILE, fold * TILE), bf16),
         v((peers, tiles, TILE, wide), bf16),
         v((tiles, TILE, 1), f32),
         v((tiles, TILE, features), bf16),
+        v((TILE, span), f32),
+        v((TILE, span), f32),
         v((two, rows), f32),
         v((2, two, rows), f32),
         v((peers, two, wide), f32),
@@ -502,10 +503,9 @@
         v((peers, probes, wide), f32),
         v((peers, probes, wide), f32),
         v((2 * two, rows), bf16),
-        v((tiles, 2 * two, TILE), bf16),
         v((2 * two, rows), bf16),
         v((peers, 2 * two, wide), bf16),
-        v((tiles, 2 * two, TILE), f32),
+        v((2 * two, rows), f32),
         v((probes, rows), f32),
         v((probes, rows), f32),
         v((probes, 128), f32),

time: 97.2 us -> 90.1 us (0.927)
  Pallas kernels: 94.8 us -> 87.7 us
    pallas_call x1, Pallas kernels: 94.8 us -> 87.7 us  [on_device(): pl.pallas_call(functools.partial(kernel, groups, devs, cap, probes, tiles...]
where the time goes in v4:
time: 90.1 us; the launch traced here: 89.9 us
  Pallas kernels  87.7 us (97%)
  other arithmetic  1.49 us (2%)
    pallas_call x1, Pallas kernels, on_device(): pl.pallas_call(functools.partial(kernel, groups, devs, cap, probes, tiles...  87.7 us

profile of v4, /device:TPU:0, one launch (start us, length us, event | category | flops | bytes accessed | tf_op | source)
XLA Modules:
  0.0 89.9 jit_solution(3601950058487220181)
XLA Ops:
  0.6 87.7 %graph_cg.1 = (f32[8,1536]{1,0:T(8,128)}, f32[8,1536]{1,0:T(8,128)}, f32[8,1536]{1,0:T(8,128)}) custom-call(s32[4,4,2,8]{3,2,1,0:T(2,128)} %bitcast.3, bf16[6,256,512]{2,1,0:T(8,128)(2,1)} %bitcast.2, f32[8,1536]{1,0:T(8,128)} %tgt.1), custom_call_target="tpu_custom_call" | custom-call | flops 9663676416 | bytes 1572864 | tf_op jit(solution)/shard_map/graph_cg/pallas_call | solution.py:521
  88.4 1.5 %fusion = (f32[8,1536]{1,0:T(8,128)}, f32[8,1536]{1,0:T(8,128)}) fusion(f32[8,1536]{1,0:T(8,128)} %get-tuple-element.5, f32[8,1536]{1,0:T(8,128)} %get-tuple-element.7, f32[8,1536]{1,0:T(8,128)} %get-tuple-element.6), kind=kLoop, calls=%fused_computation | loop fusion | flops 24576 | bytes 245760 | tf_op jit(solution)/shard_map/add | solution.py:537

commit v5 on v4

--- a/solution.py
+++ b/solution.py
@@ -173,7 +173,8 @@
             cvec(r, k).start()
 
     send_vectors(0)
-    cpts(1).start()
+    for k in range(1, groups):
+        cpts(k).start()
 
     @pl.when(even)
     def _():
@@ -184,9 +185,6 @@
     def _():
         for s in range(chunks):
             far_pts(s).start()
-
-    for k in range(2, groups):
-        cpts(k).start()
 
     def affinity(inner, norm_col, norm_row):
         dist_sq = jnp.maximum((norm_col + norm_row) + inner, 1e-30)

time: 90.1 us -> 90.1 us (level)
  no operation moved by 1% of the time
where the time goes in v5:
time: 90.1 us; the launch traced here: 89.9 us
  Pallas kernels  87.7 us (97%)
  other arithmetic  1.49 us (2%)
    pallas_call x1, Pallas kernels, on_device(): pl.pallas_call(functools.partial(kernel, groups, devs, cap, probes, tiles...  87.7 us

profile of v5, /device:TPU:0, one launch (start us, length us, event | category | flops | bytes accessed | tf_op | source)
XLA Modules:
  0.0 89.9 jit_solution(11045807605622201005)
XLA Ops:
  0.6 87.7 %graph_cg.1 = (f32[8,1536]{1,0:T(8,128)}, f32[8,1536]{1,0:T(8,128)}, f32[8,1536]{1,0:T(8,128)}) custom-call(s32[4,4,2,8]{3,2,1,0:T(2,128)} %bitcast.3, bf16[6,256,512]{2,1,0:T(8,128)(2,1)} %bitcast.2, f32[8,1536]{1,0:T(8,128)} %tgt.1), custom_call_target="tpu_custom_call" | custom-call | flops 9663676416 | bytes 1572864 | tf_op jit(solution)/shard_map/graph_cg/pallas_call | solution.py:519
  88.4 1.5 %fusion = (f32[8,1536]{1,0:T(8,128)}, f32[8,1536]{1,0:T(8,128)}) fusion(f32[8,1536]{1,0:T(8,128)} %get-tuple-element.5, f32[8,1536]{1,0:T(8,128)} %get-tuple-element.7, f32[8,1536]{1,0:T(8,128)} %get-tuple-element.6), kind=kLoop, calls=%fused_computation | loop fusion | flops 24576 | bytes 245760 | tf_op jit(solution)/shard_map/add | solution.py:535
